TPU v7x, 512 devices: a whole 4x8x8 slice. The times are simulated.
512 devices in a mesh: band: 256 (over z, x_hi, y, core), grid: 2 (over x_lo).
Axes of the slice: x: 4 (x_hi: 2, x_lo: 2; x = x_hi * 2 + x_lo), y: 8, z: 8, core: 2. Of those that a mesh axis runs over, the one named last changes fastest.
Arguments:
- orbitals: float32 [512, 64, 4096], P('band', 'grid'), may hold values from -4 to 4
- pair_list: int32 [256, 4, 2], P('band'), may hold values from 0 to 511, as said below
- pair_count: int32 [256], P('band'), may hold values from 1 to 4, 512 in all
Outputs:
- exchange_proj: float32 [512, 64, 4096], P('band', 'grid')
Inputs may be any that keep to these rules, and one draw needn't show every extreme that they name: `pair_list`: entry 0 is an orbital index 0 to 1 within the row's band group; entry 1 is a global orbital index owned by the same band group or by one of the next 2 groups, counted cyclically; the two never name the same orbital. Band group b uses its first pair_count[b] slots.
All inputs are finite; a program needn't handle non-finite values.
Results may differ from a plain program's by a relative error of at most 0.0003.
Values sent between devices are 32-bit elements; how exact they have to be, the bound alone decides.
No kernel may reach another device: no remote copies, remote signals or barrier semaphores. Data moves between devices by JAX's collectives and lax.ppermute only.
A program may use at most 64 MiB of HBM per device.

v0:
```python
import functools
import math

import jax
import jax.numpy as jnp
import ml_dtypes
import numpy as np
from jax import lax
from jax.experimental import pallas as pl
from jax.experimental.pallas import tpu as pltpu
from jax.sharding import PartitionSpec as P

SIDE = 64
TILES = SIDE // 2
LANES = 2 * SIDE
CHUNKS = 1


class Factors:
    def __init__(self, fetch, swap):
        self.fetch = fetch
        self.swap = swap


def turn(re, im, c, s):
    return re * c + im * s, im * c - re * s


def turn_back(re, im, c, s):
    return re * c - im * s, im * c + re * s


def complex_forward(re, im, size, factors):
    tiles = size // 2
    if tiles == 1:
        return [re[0], im[0]]
    half = tiles // 2
    even_re = [re[t] + re[t + half] for t in range(half)]
    even_im = [im[t] + im[t + half] for t in range(half)]
    odd_re, odd_im = [], []
    for t in range(half):
        a, b = re[t] - re[t + half], im[t] - im[t + half]
        if size == 4:
            a, b = factors.swap(a, b), factors.swap(b, -a)
        else:
            a, b = turn(a, b, *factors.fetch(size, t))
        odd_re.append(a)
        odd_im.append(b)
    return complex_forward(even_re, even_im, size // 2, factors) + complex_forward(
        odd_re, odd_im, size // 2, factors
    )


def complex_back(parts, size, factors):
    tiles = size // 2
    if tiles == 1:
        return [parts[0]], [parts[1]]
    half = tiles // 2
    even_re, even_im = complex_back(parts[:tiles], size // 2, factors)
    odd_re, odd_im = complex_back(parts[tiles:], size // 2, factors)
    low_re, low_im, high_re, high_im = [], [], [], []
    for t in range(half):
        a, b = odd_re[t], odd_im[t]
        if size == 4:
            a, b = factors.swap(a, -b), factors.swap(b, a)
        else:
            a, b = turn_back(a, b, *factors.fetch(size, t))
        low_re.append(even_re[t] + a)
        low_im.append(even_im[t] + b)
        high_re.append(even_re[t] - a)
        high_im.append(even_im[t] - b)
    return low_re + high_re, low_im + high_im


def real_forward(values, size, factors):
    tiles = size // 2
    if tiles == 1:
        return list(values)
    half = tiles // 2
    sums = [values[t] + values[t + half] for t in range(half)]
    rests = [values[t] - values[t + half] for t in range(half)]
    if size == 4:
        odd = rests
    else:
        quarter = half // 2
        re, im = [], []
        for t in range(quarter):
            a, b = turn(rests[t], -rests[t + quarter], *factors.fetch(size, t))
            re.append(a)
            im.append(b)
        odd = complex_forward(re, im, size // 4, factors)
    return real_forward(sums, size // 2, factors) + odd


def real_back(parts, size, factors):
    tiles = size // 2
    if tiles == 1:
        return list(parts)
    half = tiles // 2
    sums = real_back(parts[:half], size // 2, factors)
    if size == 4:
        rests = parts[half:]
    else:
        re, im = complex_back(parts[half:], size // 4, factors)
        quarter = half // 2
        low, high = [], []
        for t in range(quarter):
            a, b = turn_back(re[t], im[t], *factors.fetch(size, t))
            low.append(a)
            high.append(-b)
        rests = low + high
    return [sums[t] + rests[t] for t in range(half)] + [sums[t] - rests[t] for t in range(half)]


def factor_rows():
    rows, place, wanted = [], {}, []

    def note(size, t):
        if (size, t) not in wanted:
            wanted.append((size, t))
        angle = 2.0 * math.pi * (2 * t + np.arange(2)) / size
        return np.cos(angle)[:, None], np.sin(angle)[:, None]

    upper = np.array([False, True])[:, None]
    factors = Factors(note, lambda a, b: np.where(upper, b, a))
    unit = np.eye(SIDE).reshape(TILES, 2, SIDE)
    outs = real_forward([unit[t] for t in range(TILES)], SIDE, factors)
    outs = [np.stack([o[0] + o[1], o[0] - o[1]]) for o in outs]
    basis = np.concatenate(outs, 0)
    for size, t in wanted:
        angle = 2.0 * math.pi * (2 * t + np.repeat(np.arange(2), SIDE)) / size
        place[(size, t)] = len(rows)
        rows.append(np.cos(angle))
        rows.append(np.sin(angle))
    return np.stack(rows), place, basis


FACTOR_ROWS, FACTOR_PLACE, BASIS = factor_rows()


def tables():
    laplace = 2.0 * np.eye(SIDE) - np.roll(np.eye(SIDE), 1, 0) - np.roll(np.eye(SIDE), -1, 0)
    norms = np.sum(BASIS**2, 1)
    eigen_y = np.sum((BASIS @ laplace) * BASIS, 1) / norms
    points = np.arange(SIDE)
    eigen_z = 2.0 - 2.0 * np.cos(2.0 * math.pi * points / SIDE)
    mu = 1.0 / SIDE**2 + eigen_y[:, None] + eigen_z[None, :]
    ratio = 1.0 / (1.0 + mu / 2.0 + np.sqrt(mu + mu**2 / 4.0))
    scale = 1.0 / SIDE / (1.0 / ratio - ratio) / norms[:, None] / SIDE
    ratio = ratio.reshape(TILES, LANES)
    scale = scale.reshape(TILES, LANES)
    angle = 2.0 * math.pi * (points[:, None] * points[None, :] % SIDE) / SIDE
    along_z = np.cos(angle) + np.sin(angle)
    matrix = np.kron(np.array([[1.0, 1.0], [1.0, -1.0]]), along_z)
    high = matrix.astype(np.float32).astype(ml_dtypes.bfloat16)
    low = (matrix - high.astype(np.float64)).astype(ml_dtypes.bfloat16)
    row = np.concatenate([high, low], 1)
    weights = np.concatenate([row, row], 0)
    step = np.arange(8)[None, :, None]
    scans = []
    for hop in (1, 2, 4):
        scans.append(np.where(step >= hop, (ratio**hop)[:, None, :], 0.0))
    for hop in (1, 2, 4):
        scans.append(np.where(step < 8 - hop, (ratio**hop)[:, None, :], 0.0))
    spread = [ratio[:, None, :] ** (step + 1), ratio[:, None, :] ** (8 - step)]
    plain = [scale, ratio**8, ratio**32, 1.0 / (1.0 - ratio**64)]
    return (
        np.repeat(FACTOR_ROWS[:, None, :], 8, 1).astype(np.float32),
        weights,
        np.stack(scans).astype(np.float32),
        np.stack(spread).astype(np.float32),
        np.stack(plain).astype(np.float32),
    )


FACTOR_TABLE, WEIGHTS, SCAN_TABLE, SPREAD_TABLE, PLAIN_TABLE = tables()


def kernel_factors(factor_ref):
    lane = lax.broadcasted_iota(jnp.int32, (8, LANES), 1)
    upper = lane >= SIDE

    def fetch(size, t):
        at = FACTOR_PLACE[(size, t)]
        return factor_ref[at], factor_ref[at + 1]

    return Factors(fetch, lambda a, b: jnp.where(upper, b, a))


def lanes_of(t):
    return pl.ds(t * LANES, LANES)


def transform_rows(values, weights):
    high = values.astype(jnp.bfloat16)
    low = (values - high.astype(jnp.float32)).astype(jnp.bfloat16)
    both = jnp.concatenate([high, low], 1)
    out = jnp.dot(both, weights, preferred_element_type=jnp.float32)
    return out[:, :LANES] + out[:, LANES:]


def fill_window(sources, window, sems):
    copies = [
        pltpu.make_async_copy(ref, window.at[pl.ds(2 * n, 2)], sems.at[n])
        for n, ref in enumerate(sources)
    ]
    for copy in copies:
        copy.start()
    return copies


def pair_rows(ints_ref, slot):
    first = ints_ref[2 * slot]
    partner = ints_ref[2 * slot + 1]
    alive = slot < ints_ref[8]
    hop = lax.rem(partner // 2 - ints_ref[9] + ints_ref[10], ints_ref[10])
    second = 2 * hop + lax.rem(partner, 2)
    return jnp.where(alive, first, 0), jnp.where(alive, second, 0), alive


def forward_kernel(
    rows,
    ints_ref, prev_ref, own_ref, next_ref, factor_ref, weight_ref, scan_ref, plain_ref,
    local_ref, edge_ref,
    window, stage, spectrum, sems,
):
    copies = fill_window((prev_ref, own_ref, next_ref), window, sems)
    for copy in copies:
        copy.wait()
    factors = kernel_factors(factor_ref)
    octets = rows // 8

    def visit(slot, carry):
        first, second, alive = pair_rows(ints_ref, slot)
        weight = jnp.where(alive, 1.0, 0.0).astype(jnp.float32)
        for o in range(octets):
            span = pl.ds(8 * o, 8)
            values = []
            for t in range(TILES):
                left = window[first, span, lanes_of(t)]
                right = window[second, span, lanes_of(t)]
                values.append(left * right * weight)
            values = real_forward(values, SIDE, factors)
            for t in range(TILES):
                stage[o, t] = values[t]
        for o in range(octets):
            flat = stage[o].reshape(TILES * 8, LANES)
            spectrum[...] = transform_rows(flat, weight_ref[...]).reshape(TILES, 8, LANES)
            for t in range(TILES):
                value = spectrum[t] * plain_ref[0, pl.ds(t, 1), :]
                ahead = value
                behind = value
                for n, hop in enumerate((1, 2, 4)):
                    ahead = ahead + scan_ref[n, t] * pltpu.roll(ahead, hop, 0)
                    behind = behind + scan_ref[3 + n, t] * pltpu.roll(behind, 8 - hop, 0)
                local_ref[slot, o, t] = ahead + behind - value
                edge_ref[slot, o, 0, pl.ds(t, 1), :] = ahead[7:8]
                edge_ref[slot, o, 1, pl.ds(t, 1), :] = behind[0:1]
        return carry

    lax.fori_loop(0, 4, visit, 0)


def back_kernel(
    rows, begin, total,
    ints_ref, prev_ref, own_ref, next_ref, local_ref, edge_ref, other_ref,
    factor_ref, weight_ref, spread_ref, plain_ref,
    to_prev_ref, to_own_ref, to_next_ref,
    window, result, stage, fields, inflow, sems, out_sems,
):
    copies = fill_window((prev_ref, own_ref, next_ref), window, sems)
    result[...] = jnp.zeros_like(result)
    for copy in copies:
        copy.wait()
    factors = kernel_factors(factor_ref)
    octets = rows // 8

    def visit(slot, carry):
        first, second, alive = pair_rows(ints_ref, slot)
        weight = jnp.where(alive, 1.0, 0.0).astype(jnp.float32)
        step8, step32, closing = plain_ref[1], plain_ref[2], plain_ref[3]
        ahead_edges = [edge_ref[slot, o, 0] for o in range(total)]
        behind_edges = [edge_ref[slot, o, 1] for o in range(total)]

        def merged(edges):
            value = edges[0]
            for edge in edges[1:]:
                value = value * step8 + edge
            return value

        state = (other_ref[slot, 0] + step32 * merged(ahead_edges)) * closing
        for o in range(begin + octets):
            if o >= begin:
                inflow[o - begin, 0] = state
            state = state * step8 + ahead_edges[o]
        state = (other_ref[slot, 1] + step32 * merged(behind_edges[::-1])) * closing
        for o in range(total - 1, begin - 1, -1):
            if o < begin + octets:
                inflow[o - begin, 1] = state
            state = state * step8 + behind_edges[o]
        for o in range(octets):
            for t in range(TILES):
                value = local_ref[slot, o, t]
                value = value + spread_ref[0, t] * inflow[o, 0, pl.ds(t, 1), :]
                stage[t] = value + spread_ref[1, t] * inflow[o, 1, pl.ds(t, 1), :]
            flat = stage[...].reshape(TILES * 8, LANES)
            fields[...] = transform_rows(flat, weight_ref[...]).reshape(TILES, 8, LANES)
            values = real_back([fields[t] for t in range(TILES)], SIDE, factors)
            span = pl.ds(8 * o, 8)
            for t in range(TILES):
                value = values[t] * weight
                left = window[first, span, lanes_of(t)]
                right = window[second, span, lanes_of(t)]
                result[first, span, lanes_of(t)] += value * right
                result[second, span, lanes_of(t)] += value * left
        return carry

    lax.fori_loop(0, 4, visit, 0)
    copies = [
        pltpu.make_async_copy(result.at[pl.ds(2 * n, 2)], ref, out_sems.at[n])
        for n, ref in enumerate((to_prev_ref, to_own_ref, to_next_ref))
    ]
    for copy in copies:
        copy.start()
    for copy in copies:
        copy.wait()


ANY = pl.BlockSpec(memory_space=pl.ANY)
VMEM = pl.BlockSpec(memory_space=pltpu.VMEM)
SMEM = pl.BlockSpec(memory_space=pltpu.SMEM)
LIMIT = pltpu.CompilerParams(vmem_limit_bytes=48 * 1024 * 1024)


def forward(ints, prev, own, following):
    rows = own.shape[1]
    octets = rows // 8
    return pl.pallas_call(
        functools.partial(forward_kernel, rows),
        out_shape=(
            jax.ShapeDtypeStruct((4, octets, TILES, 8, LANES), jnp.float32),
            jax.ShapeDtypeStruct((4, octets, 2, TILES, LANES), jnp.float32),
        ),
        in_specs=[SMEM, ANY, ANY, ANY, VMEM, VMEM, VMEM, VMEM],
        out_specs=(VMEM, VMEM),
        scratch_shapes=[
            pltpu.VMEM((6, rows, SIDE * SIDE), jnp.float32),
            pltpu.VMEM((octets, TILES, 8, LANES), jnp.float32),
            pltpu.VMEM((TILES, 8, LANES), jnp.float32),
            pltpu.SemaphoreType.DMA((3,)),
        ],
        compiler_params=LIMIT,
        name="forward",
    )(ints, prev, own, following, FACTOR_TABLE, WEIGHTS, SCAN_TABLE, PLAIN_TABLE)


def back(ints, prev, own, following, local, edges, other, begin):
    rows = own.shape[1]
    octets = rows // 8
    block = jax.ShapeDtypeStruct(own.shape, jnp.float32)
    return pl.pallas_call(
        functools.partial(back_kernel, rows, begin, edges.shape[1]),
        out_shape=(block, block, block),
        in_specs=[SMEM, ANY, ANY, ANY, VMEM, VMEM, VMEM, VMEM, VMEM, VMEM, VMEM],
        out_specs=(ANY, ANY, ANY),
        scratch_shapes=[
            pltpu.VMEM((6, rows, SIDE * SIDE), jnp.float32),
            pltpu.VMEM((6, rows, SIDE * SIDE), jnp.float32),
            pltpu.VMEM((TILES, 8, LANES), jnp.float32),
            pltpu.VMEM((TILES, 8, LANES), jnp.float32),
            pltpu.VMEM((octets, 2, TILES, LANES), jnp.float32),
            pltpu.SemaphoreType.DMA((3,)),
            pltpu.SemaphoreType.DMA((3,)),
        ],
        compiler_params=LIMIT,
        name="back",
    )(
        ints, prev, own, following, local, edges, other,
        FACTOR_TABLE, WEIGHTS, SPREAD_TABLE, PLAIN_TABLE,
    )


def shifted(value, axis, steps):
    count = lax.axis_size(axis)
    pairs = [(source, (source + steps) % count) for source in range(count)]
    return lax.ppermute(value, axis, pairs)


def on_device(orbitals, pair_list, pair_count):
    band_count = lax.axis_size("band")
    group = lax.rem(lax.axis_index("band") + band_count - 1, band_count)
    rows = orbitals.shape[1] // CHUNKS
    own = [lax.slice_in_dim(orbitals, c * rows, (c + 1) * rows, axis=1) for c in range(CHUNKS)]
    ints = jnp.concatenate([pair_list.reshape(-1), pair_count])
    ints = shifted(ints, "band", 1)
    ints = jnp.concatenate([ints, jnp.stack([group, jnp.int32(band_count)]).astype(jnp.int32)])
    prev = [shifted(part, "band", 1) for part in own]
    following = [shifted(part, "band", -1) for part in own]
    local, edges = [], []
    for c in range(CHUNKS):
        field, edge = forward(ints, prev[c], own[c], following[c])
        local.append(field)
        edges.append(edge)
    edges = jnp.concatenate(edges, 1) if CHUNKS > 1 else edges[0]
    step8 = jnp.asarray(PLAIN_TABLE[1])
    ahead, behind = edges[:, 0, 0], edges[:, -1, 1]
    for o in range(1, edges.shape[1]):
        ahead = ahead * step8 + edges[:, o, 0]
        behind = behind * step8 + edges[:, -1 - o, 1]
    other = shifted(jnp.stack([ahead, behind], 1), "grid", 1)
    parts = []
    for c in range(CHUNKS):
        to_prev, to_own, to_next = back(
            ints, prev[c], own[c], following[c], local[c], edges, other, c * rows // 8
        )
        parts.append(to_own + shifted(to_prev, "band", -1) + shifted(to_next, "band", 1))
    return jnp.concatenate(parts, 1) if CHUNKS > 1 else parts[0]


def solution(mesh):
    in_specs = (P("band", "grid", None), P("band", None, None), P("band"))
    out_specs = P("band", "grid", None)
    return jax.shard_map(
        on_device, mesh=mesh, in_specs=in_specs, out_specs=out_specs, check_vma=False
    )
```

profile of v0, /device:TPU:2, one launch (start us, length us, event | category | flops | bytes accessed | tf_op | source)
XLA Modules:
  0.0 88.2 jit_solution(3773245336338023734)
XLA Ops:
  0.0 14.8 %collective-permute-start.2 = (f32[2,32,4096]{2,1,0:T(8,128)}, f32[2,32,4096]{2,1,0:T(8,128)S(1)}, u32[]{:S(2)}, u32[]{:S(2)}) collective-permute-start(f32[2,32,4096]{2,1,0:T(8,128)} %own_ref.3), channel_id=1, source_target_pairs={{0,510},{2,0},{4,2},{6,4},{8,6},{10,8},{12,10},{14,12},{16,14},{18... | collective-permute-start | bytes 3145736 | tf_op jit(solution)/shard_map/ppermute | solution.py:386
  14.9 1.9 %collective-permute-start.1 = (f32[2,32,4096]{2,1,0:T(8,128)}, f32[2,32,4096]{2,1,0:T(8,128)S(1)}, u32[]{:S(2)}, u32[]{:S(2)}) collective-permute-start(f32[2,32,4096]{2,1,0:T(8,128)} %own_ref.3), channel_id=1, source_target_pairs={{0,2},{2,4},{4,6},{6,8},{8,10},{10,12},{12,14},{14,16},{16,18},{18... | collective-permute-start | bytes 3145736 | tf_op jit(solution)/shard_map/ppermute | solution.py:386
  17.4 0.8 copy.19
  18.2 0.1 reshape.96
  18.3 0.1 pad_add_fusion
  18.4 1.9 %collective-permute-start = (s32[9]{0:T(128)S(1)}, s32[9]{0:T(128)S(1)}, u32[]{:S(2)}, u32[]{:S(2)}) collective-permute-start(s32[9]{0:T(128)S(1)} %pad_add_fusion), channel_id=1, source_target_pairs={{0,2},{2,4},{4,6},{6,8},{8,10},{10,12},{12,14},{14,16},{16,18},{18... | collective-permute-start | bytes 116 | tf_op jit(solution)/shard_map/ppermute | solution.py:386
  20.3 16.8 %collective-permute-done = s32[9]{0:T(128)S(1)} collective-permute-done((s32[9]{0:T(128)S(1)}, s32[9]{0:T(128)S(1)}, u32[]{:S(2)}, u32[]{:S(2)}) %collective-permute-start) | collective-permute-done | bytes 68 | tf_op jit(solution)/shard_map/ppermute | solution.py:386
  37.1 0.1 pad_add_fusion.1.ints_ref
  37.1 0.0 collective-permute-done.2.next_ref
  37.2 0.0 copy-start.1
  37.2 0.0 collective-permute-done.1.prev_ref
  37.2 0.0 copy-start
  37.2 1.6 %copy-done = f32[2,32,4096]{2,1,0:T(8,128)S(1)} copy-done((f32[2,32,4096]{2,1,0:T(8,128)S(1)}, f32[2,32,4096]{2,1,0:T(8,128)}, u32[]{:S(2)}) %copy-start) | copy-done | bytes 1048600
  38.8 0.0 copy-start.2
  38.8 1.1 %copy-done.2 = f32[6,32,8,128]{3,2,1,0:T(8,128)S(1)} copy-done((f32[6,32,8,128]{3,2,1,0:T(8,128)S(1)}, f32[6,32,8,128]{3,2,1,0:T(8,128)}, u32[]{:S(2)}) %copy-start.2) | copy-done | bytes 786456
  39.9 0.0 copy-start.3
  39.9 0.9 %copy-done.3 = f32[36,8,128]{2,1,0:T(8,128)S(1)} copy-done((f32[36,8,128]{2,1,0:T(8,128)S(1)}, f32[36,8,128]{2,1,0:T(8,128)}, u32[]{:S(2)}) %copy-start.3) | copy-done | bytes 147480
  40.8 0.0 copy-start.4
  40.8 0.9 %copy-done.4 = bf16[256,256]{1,0:T(8,128)(2,1)S(1)} copy-done((bf16[256,256]{1,0:T(8,128)(2,1)S(1)}, bf16[256,256]{1,0:T(8,128)(2,1)}, u32[]{:S(2)}) %copy-start.4) | copy-done | bytes 131096
  41.7 0.0 copy-start.5
  41.7 0.8 copy-done.5
  42.6 0.0 copy-start.7
  42.6 0.0 copy-start.6
  42.6 5.1 %forward.1 = (f32[4,4,32,8,128]{4,3,2,1,0:T(8,128)}, f32[4,4,2,32,128]{4,3,2,1,0:T(8,128)S(1)}) custom-call(s32[11]{0:T(128)S(1)} %pad_add_fusion.1.ints_ref, f32[2,32,4096]{2,1,0:T(8,128)S(1)} %collective-permute-done.1.prev_ref, f32[2,32,4096]{2,1,0:T(8,128)S(1)} %copy-done, f32[2,32,4096]{2,1,0:T(8,128)S(1)} %collective-permute-done.2.next_ref, ...), custom_call_target="tpu_custom_call" | custom-call | tf_op jit(solution)/shard_map/forward/pallas_call | solution.py:338
  47.6 0.0 copy-done.1
  47.6 0.0 copy-done.7
  47.7 3.3 %collective-permute-start.3 = (f32[4,2,32,128]{3,2,1,0:T(8,128)S(1)}, f32[4,2,32,128]{3,2,1,0:T(8,128)S(1)}, u32[]{:S(2)}, u32[]{:S(2)}) collective-permute-start(f32[4,2,32,128]{3,2,1,0:T(8,128)S(1)} %pad_maximum_fusion), channel_id=1, source_target_pairs={{0,1},{1,0},{2,3},{3,2},{4,5},{5,4},{6,7},{7,6},{8,9},{9,8},{10,11... | collective-permute-start | bytes 393224 | tf_op jit(solution)/shard_map/ppermute | solution.py:386
  51.1 3.5 %collective-permute-done.3.other_ref = f32[4,2,32,128]{3,2,1,0:T(8,128)S(1)} collective-permute-done((f32[4,2,32,128]{3,2,1,0:T(8,128)S(1)}, f32[4,2,32,128]{3,2,1,0:T(8,128)S(1)}, u32[]{:S(2)}, u32[]{:S(2)}) %collective-permute-start.3) | collective-permute-done | bytes 131104 | tf_op jit(solution)/shard_map/ppermute | solution.py:386
  54.6 0.0 copy-done.6
  54.6 8.7 %back.1 = (f32[2,32,4096]{2,1,0:T(8,128)S(1)}, f32[2,32,4096]{2,1,0:T(8,128)S(1)}, f32[2,32,4096]{2,1,0:T(8,128)S(1)}) custom-call(s32[11]{0:T(128)S(1)} %pad_add_fusion.1.ints_ref, f32[2,32,4096]{2,1,0:T(8,128)S(1)} %collective-permute-done.1.prev_ref, f32[2,32,4096]{2,1,0:T(8,128)} %own_ref.3, f32[2,32,4096]{2,1,0:T(8,128)} %copy-done.1, ...), custom_call_target="tpu_custom_call" | custom-call | tf_op jit(solution)/shard_map/back/pallas_call | solution.py:361
  63.3 1.9 %collective-permute-start.4 = (f32[2,32,4096]{2,1,0:T(8,128)S(1)}, f32[2,32,4096]{2,1,0:T(8,128)S(1)}, u32[]{:S(2)}, u32[]{:S(2)}) collective-permute-start(f32[2,32,4096]{2,1,0:T(8,128)S(1)} %get-tuple-element.13), channel_id=1, source_target_pairs={{0,510},{2,0},{4,2},{6,4},{8,6},{10,8},{12,10},{14,12},{16,14},{18... | collective-permute-start | bytes 3145736 | tf_op jit(solution)/shard_map/ppermute | solution.py:386
  65.2 2.4 %collective-permute-start.5 = (f32[2,32,4096]{2,1,0:T(8,128)S(1)}, f32[2,32,4096]{2,1,0:T(8,128)S(1)}, u32[]{:S(2)}, u32[]{:S(2)}) collective-permute-start(f32[2,32,4096]{2,1,0:T(8,128)S(1)} %get-tuple-element.14), channel_id=1, source_target_pairs={{0,2},{2,4},{4,6},{6,8},{8,10},{10,12},{12,14},{14,16},{16,18},{18... | collective-permute-start | bytes 3145736 | tf_op jit(solution)/shard_map/ppermute | solution.py:386
  67.6 9.9 %collective-permute-done.4 = f32[2,32,4096]{2,1,0:T(8,128)S(1)} collective-permute-done((f32[2,32,4096]{2,1,0:T(8,128)S(1)}, f32[2,32,4096]{2,1,0:T(8,128)S(1)}, u32[]{:S(2)}, u32[]{:S(2)}) %collective-permute-start.4) | collective-permute-done | bytes 1048608 | tf_op jit(solution)/shard_map/ppermute | solution.py:386
  77.5 9.5 %collective-permute-done.5 = f32[2,32,4096]{2,1,0:T(8,128)S(1)} collective-permute-done((f32[2,32,4096]{2,1,0:T(8,128)S(1)}, f32[2,32,4096]{2,1,0:T(8,128)S(1)}, u32[]{:S(2)}, u32[]{:S(2)}) %collective-permute-start.5) | collective-permute-done | bytes 1048608 | tf_op jit(solution)/shard_map/ppermute | solution.py:386
  87.1 1.2 %add_add_fusion = f32[2,32,4096]{2,1,0:T(8,128)} fusion(f32[2,32,4096]{2,1,0:T(8,128)S(1)} %collective-permute-done.5, f32[2,32,4096]{2,1,0:T(8,128)S(1)} %get-tuple-element.12, f32[2,32,4096]{2,1,0:T(8,128)S(1)} %collective-permute-done.4), kind=kLoop, calls=%fused_computation | loop fusion | flops 524288 | bytes 4194304 | tf_op jit(solution)/shard_map/add | solution.py:416
  (2 shorter events, 0.1 us)
Async XLA Ops:
  0.0 37.1 %collective-permute-start.2 = (f32[2,32,4096]{2,1,0:T(8,128)}, f32[2,32,4096]{2,1,0:T(8,128)S(1)}, u32[]{:S(2)}, u32[]{:S(2)}) collective-permute-start(f32[2,32,4096]{2,1,0:T(8,128)} %own_ref.3), channel_id=1, source_target_pairs={{0,510},{2,0},{4,2},{6,4},{8,6},{10,8},{12,10},{14,12},{16,14},{18... | collective-permute-start | bytes 3145736 | tf_op jit(solution)/shard_map/ppermute | solution.py:386
  14.9 22.3 %collective-permute-start.1 = (f32[2,32,4096]{2,1,0:T(8,128)}, f32[2,32,4096]{2,1,0:T(8,128)S(1)}, u32[]{:S(2)}, u32[]{:S(2)}) collective-permute-start(f32[2,32,4096]{2,1,0:T(8,128)} %own_ref.3), channel_id=1, source_target_pairs={{0,2},{2,4},{4,6},{6,8},{8,10},{10,12},{12,14},{14,16},{16,18},{18... | collective-permute-start | bytes 3145736 | tf_op jit(solution)/shard_map/ppermute | solution.py:386
  18.4 18.7 %collective-permute-start = (s32[9]{0:T(128)S(1)}, s32[9]{0:T(128)S(1)}, u32[]{:S(2)}, u32[]{:S(2)}) collective-permute-start(s32[9]{0:T(128)S(1)} %pad_add_fusion), channel_id=1, source_target_pairs={{0,2},{2,4},{4,6},{6,8},{8,10},{10,12},{12,14},{14,16},{16,18},{18... | collective-permute-start | bytes 116 | tf_op jit(solution)/shard_map/ppermute | solution.py:386
  37.2 10.5 %copy-start.1 = (f32[2,32,4096]{2,1,0:T(8,128)}, f32[2,32,4096]{2,1,0:T(8,128)S(1)}, u32[]{:S(2)}) copy-start(f32[2,32,4096]{2,1,0:T(8,128)S(1)} %collective-permute-done.2.next_ref) | copy-start | bytes 3145732
  37.2 1.6 %copy-start = (f32[2,32,4096]{2,1,0:T(8,128)S(1)}, f32[2,32,4096]{2,1,0:T(8,128)}, u32[]{:S(2)}) copy-start(f32[2,32,4096]{2,1,0:T(8,128)} %own_ref.3) | copy-start | bytes 3145732
  38.8 1.1 %copy-start.2 = (f32[6,32,8,128]{3,2,1,0:T(8,128)S(1)}, f32[6,32,8,128]{3,2,1,0:T(8,128)}, u32[]{:S(2)}) copy-start(f32[6,32,8,128]{3,2,1,0:T(8,128)} %constant.30.clone.scan_ref) | copy-start | bytes 2359300
  39.9 0.9 %copy-start.3 = (f32[36,8,128]{2,1,0:T(8,128)S(1)}, f32[36,8,128]{2,1,0:T(8,128)}, u32[]{:S(2)}) copy-start(f32[36,8,128]{2,1,0:T(8,128)} %constant.28.clone.factor_ref) | copy-start | bytes 442372
  40.8 0.9 %copy-start.4 = (bf16[256,256]{1,0:T(8,128)(2,1)S(1)}, bf16[256,256]{1,0:T(8,128)(2,1)}, u32[]{:S(2)}) copy-start(bf16[256,256]{1,0:T(8,128)(2,1)} %constant.29.clone.weight_ref) | copy-start | bytes 393220
  41.7 0.8 copy-start.5
  42.6 5.1 %copy-start.7 = (f32[32,128]{1,0:T(8,128)S(1)}, f32[32,128]{1,0:T(8,128)}, u32[]{:S(2)}) copy-start(f32[32,128]{1,0:T(8,128)} %constant.32.clone) | copy-start | bytes 49156
  42.6 12.0 %copy-start.6 = (f32[2,32,8,128]{3,2,1,0:T(8,128)S(1)}, f32[2,32,8,128]{3,2,1,0:T(8,128)}, u32[]{:S(2)}) copy-start(f32[2,32,8,128]{3,2,1,0:T(8,128)} %constant.33.clone.spread_ref) | copy-start | bytes 786436
  47.7 6.9 %collective-permute-start.3 = (f32[4,2,32,128]{3,2,1,0:T(8,128)S(1)}, f32[4,2,32,128]{3,2,1,0:T(8,128)S(1)}, u32[]{:S(2)}, u32[]{:S(2)}) collective-permute-start(f32[4,2,32,128]{3,2,1,0:T(8,128)S(1)} %pad_maximum_fusion), channel_id=1, source_target_pairs={{0,1},{1,0},{2,3},{3,2},{4,5},{5,4},{6,7},{7,6},{8,9},{9,8},{10,11... | collective-permute-start | bytes 393224 | tf_op jit(solution)/shard_map/ppermute | solution.py:386
  63.3 14.2 %collective-permute-start.4 = (f32[2,32,4096]{2,1,0:T(8,128)S(1)}, f32[2,32,4096]{2,1,0:T(8,128)S(1)}, u32[]{:S(2)}, u32[]{:S(2)}) collective-permute-start(f32[2,32,4096]{2,1,0:T(8,128)S(1)} %get-tuple-element.13), channel_id=1, source_target_pairs={{0,510},{2,0},{4,2},{6,4},{8,6},{10,8},{12,10},{14,12},{16,14},{18... | collective-permute-start | bytes 3145736 | tf_op jit(solution)/shard_map/ppermute | solution.py:386
  65.2 21.8 %collective-permute-start.5 = (f32[2,32,4096]{2,1,0:T(8,128)S(1)}, f32[2,32,4096]{2,1,0:T(8,128)S(1)}, u32[]{:S(2)}, u32[]{:S(2)}) collective-permute-start(f32[2,32,4096]{2,1,0:T(8,128)S(1)} %get-tuple-element.14), channel_id=1, source_target_pairs={{0,2},{2,4},{4,6},{6,8},{8,10},{10,12},{12,14},{14,16},{16,18},{18... | collective-permute-start | bytes 3145736 | tf_op jit(solution)/shard_map/ppermute | solution.py:386
where the time goes:
time: 88.7 us; the launch traced here: 88.2 us
  waiting for transfers between devices  39.7 us (45%)
  starting transfers between devices  26.3 us (30%)
  Pallas kernels  13.8 us (16%)
  local copies, waits for them, and re-layouts  6.24 us (7%)
  other arithmetic  1.37 us (2%)
    ppermute x6, waiting for transfers between devices, shifted(): return lax.ppermute(value, axis, pairs)  39.7 us
    ppermute x6, starting transfers between devices, shifted(): return lax.ppermute(value, axis, pairs)  26.3 us
    pallas_call x1, Pallas kernels, back(): pl.pallas_call(functools.partial(back_kernel, rows, begin, edges.shape[1]...  8.71 us
    unnamed x17, local copies, waits for them, and re-layouts  6.16 us
    pallas_call x1, Pallas kernels, forward(): pl.pallas_call(functools.partial(forward_kernel, rows), out_shape=(jax.Sh...  5.06 us
  transfers between devices with their start and end apart: 6, of which 4 were waited for; matrix products, arithmetic and copies ran while one was open for 1% of the time, Pallas kernels for 0%

commit v1 on v0

v1 whole, which is shorter than its diff:
```python
import functools
import math

import jax
import jax.numpy as jnp
import ml_dtypes
import numpy as np
from jax import lax
from jax.experimental import pallas as pl
from jax.experimental.pallas import tpu as pltpu
from jax.sharding import PartitionSpec as P

SIDE = 64
TILES = SIDE // 2
LANES = 2 * SIDE
BACK_CHUNKS = 1
GROUPS = TILES // 8
FACTORS = 36


class Factors:
    def __init__(self, fetch, swap):
        self.fetch = fetch
        self.swap = swap


def turn(re, im, c, s):
    return re * c + im * s, im * c - re * s


def turn_back(re, im, c, s):
    return re * c - im * s, im * c + re * s


def complex_forward(re, im, size, factors):
    tiles = size // 2
    if tiles == 1:
        return [re[0], im[0]]
    half = tiles // 2
    even_re = [re[t] + re[t + half] for t in range(half)]
    even_im = [im[t] + im[t + half] for t in range(half)]
    odd_re, odd_im = [], []
    for t in range(half):
        a, b = re[t] - re[t + half], im[t] - im[t + half]
        if size == 4:
            a, b = factors.swap(a, b), factors.swap(b, -a)
        else:
            a, b = turn(a, b, *factors.fetch(size, t))
        odd_re.append(a)
        odd_im.append(b)
    return complex_forward(even_re, even_im, size // 2, factors) + complex_forward(
        odd_re, odd_im, size // 2, factors
    )


def complex_back(parts, size, factors):
    tiles = size // 2
    if tiles == 1:
        return [parts[0]], [parts[1]]
    half = tiles // 2
    even_re, even_im = complex_back(parts[:tiles], size // 2, factors)
    odd_re, odd_im = complex_back(parts[tiles:], size // 2, factors)
    low_re, low_im, high_re, high_im = [], [], [], []
    for t in range(half):
        a, b = odd_re[t], odd_im[t]
        if size == 4:
            a, b = factors.swap(a, -b), factors.swap(b, a)
        else:
            a, b = turn_back(a, b, *factors.fetch(size, t))
        low_re.append(even_re[t] + a)
        low_im.append(even_im[t] + b)
        high_re.append(even_re[t] - a)
        high_im.append(even_im[t] - b)
    return low_re + high_re, low_im + high_im


def real_forward(values, size, factors):
    tiles = size // 2
    if tiles == 1:
        return list(values)
    half = tiles // 2
    sums = [values[t] + values[t + half] for t in range(half)]
    rests = [values[t] - values[t + half] for t in range(half)]
    if size == 4:
        odd = rests
    else:
        quarter = half // 2
        re, im = [], []
        for t in range(quarter):
            a, b = turn(rests[t], -rests[t + quarter], *factors.fetch(size, t))
            re.append(a)
            im.append(b)
        odd = complex_forward(re, im, size // 4, factors)
    return real_forward(sums, size // 2, factors) + odd


def real_back(parts, size, factors):
    tiles = size // 2
    if tiles == 1:
        return list(parts)
    half = tiles // 2
    sums = real_back(parts[:half], size // 2, factors)
    if size == 4:
        rests = parts[half:]
    else:
        re, im = complex_back(parts[half:], size // 4, factors)
        quarter = half // 2
        low, high = [], []
        for t in range(quarter):
            a, b = turn_back(re[t], im[t], *factors.fetch(size, t))
            low.append(a)
            high.append(-b)
        rests = low + high
    return [sums[t] + rests[t] for t in range(half)] + [sums[t] - rests[t] for t in range(half)]


def factor_rows():
    rows, place, wanted = [], {}, []

    def note(size, t):
        if (size, t) not in wanted:
            wanted.append((size, t))
        angle = 2.0 * math.pi * (2 * t + np.arange(2)) / size
        return np.cos(angle)[:, None], np.sin(angle)[:, None]

    upper = np.array([False, True])[:, None]
    factors = Factors(note, lambda a, b: np.where(upper, b, a))
    unit = np.eye(SIDE).reshape(TILES, 2, SIDE)
    outs = real_forward([unit[t] for t in range(TILES)], SIDE, factors)
    outs = [np.stack([o[0] + o[1], o[0] - o[1]]) for o in outs]
    basis = np.concatenate(outs, 0)
    for size, t in wanted:
        angle = 2.0 * math.pi * (2 * t + np.repeat(np.arange(2), SIDE)) / size
        place[(size, t)] = len(rows)
        rows.append(np.cos(angle))
        rows.append(np.sin(angle))
    return np.stack(rows), place, basis


FACTOR_ROWS, FACTOR_PLACE, BASIS = factor_rows()


def tables():
    laplace = 2.0 * np.eye(SIDE) - np.roll(np.eye(SIDE), 1, 0) - np.roll(np.eye(SIDE), -1, 0)
    norms = np.sum(BASIS**2, 1)
    eigen_y = np.sum((BASIS @ laplace) * BASIS, 1) / norms
    points = np.arange(SIDE)
    eigen_z = 2.0 - 2.0 * np.cos(2.0 * math.pi * points / SIDE)
    mu = 1.0 / SIDE**2 + eigen_y[:, None] + eigen_z[None, :]
    ratio = 1.0 / (1.0 + mu / 2.0 + np.sqrt(mu + mu**2 / 4.0))
    scale = 1.0 / SIDE / (1.0 / ratio - ratio) / norms[:, None] / SIDE
    ratio = ratio.reshape(TILES, LANES)
    scale = scale.reshape(TILES, LANES)
    angle = 2.0 * math.pi * (points[:, None] * points[None, :] % SIDE) / SIDE
    along_z = np.cos(angle) + np.sin(angle)
    matrix = np.kron(np.array([[1.0, 1.0], [1.0, -1.0]]), along_z)
    high = matrix.astype(np.float32).astype(ml_dtypes.bfloat16)
    low = (matrix - high.astype(np.float64)).astype(ml_dtypes.bfloat16)
    row = np.concatenate([high, low], 1)
    weights = np.concatenate([row, row], 0)
    rows = SIDE // 2 // BACK_CHUNKS
    plain = np.stack([ratio, scale, ratio**rows, ratio**32, 1.0 / (1.0 - ratio**64)])
    factors = np.repeat(FACTOR_ROWS[:, None, :], 8, 1)
    table = np.concatenate([factors, plain.reshape(-1, 8, LANES)], 0)
    return weights, table.astype(np.float32)


WEIGHTS, TABLE = tables()
assert len(FACTOR_ROWS) == FACTORS


def kernel_factors(table_ref):
    lane = lax.broadcasted_iota(jnp.int32, (8, LANES), 1)
    upper = lane >= SIDE

    def fetch(size, t):
        at = FACTOR_PLACE[(size, t)]
        return table_ref[at], table_ref[at + 1]

    return Factors(fetch, lambda a, b: jnp.where(upper, b, a))


def plain(table_ref, kind, group):
    return table_ref[FACTORS + GROUPS * kind + group]


def lanes_of(t):
    return pl.ds(t * LANES, LANES)


def transform_rows(values, weights):
    high = values.astype(jnp.bfloat16)
    low = (values - high.astype(jnp.float32)).astype(jnp.bfloat16)
    both = jnp.concatenate([high, low], 1)
    out = jnp.dot(both, weights, preferred_element_type=jnp.float32)
    return out[:, :LANES] + out[:, LANES:]


def pair_rows(ints_ref, slot):
    groups = lax.axis_size("band")
    below = lax.axis_index("band") + groups - 1
    first = ints_ref[2 * slot]
    partner = ints_ref[2 * slot + 1]
    alive = slot < ints_ref[8]
    hop = lax.rem(partner // 2 - lax.rem(below, groups) + groups, groups)
    second = 2 * hop + lax.rem(partner, 2)
    return jnp.where(alive, first, 0), jnp.where(alive, second, 0), alive


def cross_at():
    return 4 * lax.rem(lax.axis_index("band"), 2)


def prepare_kernel(
    pairs_ref, count_ref, own_ref, weight_ref, table_ref,
    ints_ref, window, weights, table, sems,
):
    copies = [
        pltpu.make_async_copy(own_ref, window.at[pl.ds(2, 2)], sems.at[0]),
        pltpu.make_async_copy(weight_ref, weights, sems.at[1]),
        pltpu.make_async_copy(table_ref, table, sems.at[2]),
    ]
    for copy in copies:
        copy.start()
    for n in range(4):
        ints_ref[2 * n] = pairs_ref[0, n, 0]
        ints_ref[2 * n + 1] = pairs_ref[0, n, 1]
    ints_ref[8] = count_ref[0]
    for copy in copies:
        copy.wait()


def forward_kernel(
    ints_ref, mate_ref, cross_ref, window_ref, weights, table,
    local_ref, edge_ref, window,
    stage, sems,
):
    rows = window.shape[1]
    cross = cross_at()
    copies = [
        pltpu.make_async_copy(mate_ref, window.at[pl.ds(4 - cross, 2)], sems.at[0]),
        pltpu.make_async_copy(cross_ref, window.at[pl.ds(cross, 2)], sems.at[1]),
    ]
    for copy in copies:
        copy.start()
    for copy in copies:
        copy.wait()
    factors = kernel_factors(table)

    def along_y(slot):
        first, second, alive = pair_rows(ints_ref, slot)
        for o in range(rows // 8):
            values = []
            for t in range(TILES):
                left = window[first, pl.ds(8 * o, 8), lanes_of(t)]
                right = window[second, pl.ds(8 * o, 8), lanes_of(t)]
                values.append(left * right)
            values = real_forward(values, SIDE, factors)
            for t in range(TILES):
                stage[slot, pl.ds((o * TILES + t) * 8, 8)] = values[t]

    def along_zx(slot, g):
        alive = pair_rows(ints_ref, slot)[2]
        weight = jnp.where(alive, 1.0, 0.0).astype(jnp.float32)
        parts = [
            stage[slot, pl.ds(x // 8 * TILES * 8 + g * 64 + x % 8, 8, stride=8)]
            for x in range(rows)
        ]
        spectrum = transform_rows(jnp.concatenate(parts, 0), weights[...])
        ratio, scale = plain(table, 0, g), plain(table, 1, g) * weight
        values = [spectrum[8 * x : 8 * x + 8] * scale for x in range(rows)]
        ahead = values[0]
        sums = [ahead]
        for x in range(1, rows):
            ahead = ahead * ratio
            sums.append(ahead)
            ahead = ahead + values[x]
        behind = values[rows - 1]
        local_ref[slot, g, rows - 1] = sums[rows - 1] + behind
        for x in range(rows - 2, -1, -1):
            behind = behind * ratio + values[x]
            local_ref[slot, g, x] = (sums[x] + behind) if x else behind
        edge_ref[slot, 0, g] = ahead
        edge_ref[slot, 1, g] = behind

    along_y(0)
    for slot in range(4):
        if slot < 3:
            along_y(slot + 1)
        for g in range(GROUPS):
            along_zx(slot, g)


def back_kernel(
    rows, chunk,
    ints_ref, window, local_ref, edge_ref, other_ref, weights, table, *rest,
):
    if chunk:
        rest = rest[2:]
    cross_ref, mate_ref, own_ref, result, fields, out_sems = rest
    cross = cross_at()
    begin = chunk * rows
    result[...] = jnp.zeros_like(result)
    factors = kernel_factors(table)

    def along_xz(slot, g):
        ratio, step = plain(table, 0, g), plain(table, 2, g)
        whole, closing = plain(table, 3, g), plain(table, 4, g)
        ahead = (other_ref[slot, 0, g] + whole * edge_ref[slot, 0, g]) * closing
        for _ in range(chunk):
            ahead = ahead * step
        behind = (other_ref[slot, 1, g] + whole * edge_ref[slot, 1, g]) * closing
        for _ in range(BACK_CHUNKS - 1 - chunk):
            behind = behind * step
        behinds = []
        for x in range(rows):
            behind = behind * ratio
            behinds.append(behind)
        parts = []
        for x in range(rows):
            ahead = ahead * ratio
            parts.append(local_ref[slot, g, begin + x] + (ahead + behinds[rows - 1 - x]))
        values = transform_rows(jnp.concatenate(parts, 0), weights[...])
        for x in range(rows):
            fields[slot, pl.ds(x * TILES + 8 * g, 8)] = values[8 * x : 8 * x + 8]

    def along_y(slot):
        first, second, alive = pair_rows(ints_ref, slot)
        for o in range(rows // 8):
            values = [
                fields[slot, pl.ds(8 * o * TILES + t, 8, stride=TILES)] for t in range(TILES)
            ]
            values = real_back(values, SIDE, factors)
            here = pl.ds(8 * o, 8)
            there = pl.ds(begin + 8 * o, 8)
            for begin_t in range(0, TILES, 8):
                new = []
                for t in range(begin_t, begin_t + 8):
                    left = window[first, there, lanes_of(t)]
                    right = window[second, there, lanes_of(t)]
                    new.append((
                        result[first, here, lanes_of(t)] + values[t] * right,
                        result[second, here, lanes_of(t)] + values[t] * left,
                    ))
                for t in range(begin_t, begin_t + 8):
                    result[first, here, lanes_of(t)] = new[t - begin_t][0]
                for t in range(begin_t, begin_t + 8):
                    result[second, here, lanes_of(t)] = new[t - begin_t][1]

    for slot in range(5):
        if slot < 4:
            for g in range(GROUPS):
                along_xz(slot, g)
        if slot:
            along_y(slot - 1)
    span = pl.ds(begin, rows)
    copies = [
        pltpu.make_async_copy(result.at[pl.ds(cross, 2)], cross_ref, out_sems.at[0]),
        pltpu.make_async_copy(result.at[pl.ds(4 - cross, 2)], mate_ref.at[:, span], out_sems.at[1]),
        pltpu.make_async_copy(result.at[pl.ds(2, 2)], own_ref.at[:, span], out_sems.at[2]),
    ]
    for copy in copies:
        copy.start()
    for copy in copies:
        copy.wait()


ANY = pl.BlockSpec(memory_space=pl.ANY)
HBM = pl.BlockSpec(memory_space=pltpu.HBM)
VMEM = pl.BlockSpec(memory_space=pltpu.VMEM)
SMEM = pl.BlockSpec(memory_space=pltpu.SMEM)
LIMIT = pltpu.CompilerParams(vmem_limit_bytes=20 * 1024 * 1024)
COST = pl.CostEstimate(flops=0, bytes_accessed=12_000_000, transcendentals=0)


def prepare(pair_list, pair_count, own):
    rows = own.shape[1]
    return pl.pallas_call(
        prepare_kernel,
        out_shape=(
            jax.ShapeDtypeStruct((9,), jnp.int32),
            jax.ShapeDtypeStruct((6, rows, SIDE * SIDE), jnp.float32),
            jax.ShapeDtypeStruct(WEIGHTS.shape, jnp.bfloat16),
            jax.ShapeDtypeStruct(TABLE.shape, jnp.float32),
        ),
        in_specs=[SMEM, SMEM, HBM, HBM, HBM],
        out_specs=(SMEM, VMEM, VMEM, VMEM),
        scratch_shapes=[pltpu.SemaphoreType.DMA((3,))],
        compiler_params=LIMIT,
        name="prepare",
    )(pair_list, pair_count, own, WEIGHTS, TABLE)


def forward(ints, mate, cross, window, weights, table):
    rows = window.shape[1]
    return pl.pallas_call(
        forward_kernel,
        out_shape=(
            jax.ShapeDtypeStruct((4, GROUPS, rows, 8, LANES), jnp.float32),
            jax.ShapeDtypeStruct((4, 2, GROUPS, 8, LANES), jnp.float32),
            jax.ShapeDtypeStruct((6, rows, SIDE * SIDE), jnp.float32),
        ),
        in_specs=[SMEM, ANY, ANY, VMEM, VMEM, VMEM],
        out_specs=(VMEM, VMEM, VMEM),
        input_output_aliases={3: 2},
        scratch_shapes=[
            pltpu.VMEM((4, rows * TILES, LANES), jnp.float32),
            pltpu.SemaphoreType.DMA((2,)),
        ],
        compiler_params=LIMIT,
        cost_estimate=COST,
        name="forward",
    )(ints, mate, cross, window, weights, table)


def back(ints, window, local, edges, other, weights, table, chunk, carried):
    rows = window.shape[1] // BACK_CHUNKS
    part = jax.ShapeDtypeStruct((2, rows, SIDE * SIDE), jnp.float32)
    block = jax.ShapeDtypeStruct((2, rows * BACK_CHUNKS, SIDE * SIDE), jnp.float32)
    return pl.pallas_call(
        functools.partial(back_kernel, rows, chunk),
        out_shape=(part, block, block),
        in_specs=[SMEM] + [VMEM] * 6 + [ANY] * len(carried),
        out_specs=(ANY, ANY, ANY),
        input_output_aliases={7: 1, 8: 2} if carried else {},
        scratch_shapes=[
            pltpu.VMEM((6, rows, SIDE * SIDE), jnp.float32),
            pltpu.VMEM((4, rows * TILES, LANES), jnp.float32),
            pltpu.SemaphoreType.DMA((3,)),
        ],
        compiler_params=LIMIT,
        cost_estimate=COST,
        name="back",
    )(ints, window, local, edges, other, weights, table, *carried)


def moved(value, axis, target):
    count = lax.axis_size(axis)
    return lax.ppermute(value, axis, [(n, target(n) % count) for n in range(count)])


def to_mate(value):
    return moved(value, "band", lambda n: n ^ 1)


def to_cross(value):
    return moved(value, "band", lambda n: n + 1 if n % 2 else n - 1)


def on_device(orbitals, pair_list, pair_count):
    cross = to_cross(orbitals)
    ints, window, weights, table = prepare(pair_list, pair_count, orbitals)
    held, ints = lax.optimization_barrier((orbitals, ints))
    ints = moved(ints, "band", lambda n: n + 1)
    mate = to_mate(held)
    local, edges, window = forward(ints, mate, cross, window, weights, table)
    other = moved(edges, "grid", lambda n: n + 1)
    returned, carried = [], ()
    for chunk in range(BACK_CHUNKS):
        part, *carried = back(ints, window, local, edges, other, weights, table, chunk, carried)
        returned.append(to_cross(part))
    mate, own = carried
    return (own + returned[0]) + to_mate(mate)


def solution(mesh):
    in_specs = (P("band", "grid", None), P("band", None, None), P("band"))
    out_specs = P("band", "grid", None)
    return jax.shard_map(
        on_device, mesh=mesh, in_specs=in_specs, out_specs=out_specs, check_vma=False
    )
```

time: 88.7 us -> 70.8 us (0.80)
  waiting for transfers between devices: 39.7 us -> 29.4 us
  Pallas kernels: 13.8 us -> 8.67 us
  local copies, waits for them, and re-layouts: 6.24 us -> 3.83 us
    ppermute x6, waiting for transfers between devices: 39.7 us -> 29.4 us  [moved(): lax.ppermute(value, axis, [(n, target(n) % count) for n in range(count)])]
    pallas_call x2 -> x3, Pallas kernels: 13.8 us -> 8.67 us  [the longest x1 4.08 us: back(): pl.pallas_call(functools.partial(back_kernel, rows, chunk), out_shape=(pa...]
    unnamed x17 -> x7, local copies, waits for them, and re-layouts: 6.16 us -> 3.83 us
  transfers between devices with their start and end apart: 6 -> 6, of which waited for: 4 -> 3; matrix products, arithmetic and copies ran while one was open for 1% -> 1% of each run, Pallas kernels for 0% -> 2%
where the time goes in v1:
time: 70.8 us; the launch traced here: 70.4 us
  waiting for transfers between devices  29.4 us (42%)
  starting transfers between devices  26.6 us (38%)
  Pallas kernels  8.67 us (12%)
  local copies, waits for them, and re-layouts  3.83 us (5%)
  other arithmetic  1.17 us (2%)
  between operations  0.72 us (1%)
    ppermute x6, waiting for transfers between devices, moved(): lax.ppermute(value, axis, [(n, target(n) % count) for n in range(count)])  29.4 us
    ppermute x6, starting transfers between devices, moved(): lax.ppermute(value, axis, [(n, target(n) % count) for n in range(count)])  26.6 us
    pallas_call x1, Pallas kernels, back(): pl.pallas_call(functools.partial(back_kernel, rows, chunk), out_shape=(pa...  4.08 us
    unnamed x7, local copies, waits for them, and re-layouts  3.83 us
    pallas_call x1, Pallas kernels, forward(): pl.pallas_call(forward_kernel, out_shape=(jax.ShapeDtypeStruct((4, GROUPS...  2.86 us
    pallas_call x1, Pallas kernels, prepare(): pl.pallas_call(prepare_kernel, out_shape=(jax.ShapeDtypeStruct((9,), jnp....  1.73 us
  transfers between devices with their start and end apart: 6, of which 3 were waited for; matrix products, arithmetic and copies ran while one was open for 1% of the time, Pallas kernels for 2%

profile of v1, /device:TPU:2, one launch (start us, length us, event | category | flops | bytes accessed | tf_op | source)
XLA Modules:
  0.0 70.4 jit_solution(15353083919672532387)
XLA Ops:
  0.0 14.8 %collective-permute-start.2 = (f32[2,32,4096]{2,1,0:T(8,128)}, f32[2,32,4096]{2,1,0:T(8,128)S(1)}, u32[]{:S(2)}, u32[]{:S(2)}) collective-permute-start(f32[2,32,4096]{2,1,0:T(8,128)} %own_ref.1), channel_id=1, source_target_pairs={{0,510},{2,4},{4,2},{6,8},{8,6},{10,12},{12,10},{14,16},{16,14},{1... | collective-permute-start | bytes 3145736 | tf_op jit(solution)/shard_map/ppermute | solution.py:439
  15.5 0.8 %copy.7.pairs_ref = s32[1,4,2]{2,1,0:T(4,128)S(1)} copy(s32[1,4,2]{1,2,0:T(2,128)} %param.6) | data formatting | bytes 64 | tf_op args[1]
  16.3 0.0 copy-start
  16.3 1.2 %copy-done = f32[2,32,4096]{2,1,0:T(8,128)S(1)} copy-done((f32[2,32,4096]{2,1,0:T(8,128)S(1)}, f32[2,32,4096]{2,1,0:T(8,128)}, u32[]{:S(2)}) %copy-start) | copy-done | bytes 1048600
  17.5 0.0 copy-start.1
  17.5 0.9 %copy-done.1 = f32[56,8,128]{2,1,0:T(8,128)S(1)} copy-done((f32[56,8,128]{2,1,0:T(8,128)S(1)}, f32[56,8,128]{2,1,0:T(8,128)}, u32[]{:S(2)}) %copy-start.1) | copy-done | bytes 229400
  18.4 0.0 copy-start.2
  18.4 0.9 %copy-done.2 = bf16[256,256]{1,0:T(8,128)(2,1)S(1)} copy-done((bf16[256,256]{1,0:T(8,128)(2,1)S(1)}, bf16[256,256]{1,0:T(8,128)(2,1)}, u32[]{:S(2)}) %copy-start.2) | copy-done | bytes 131096
  19.3 1.7 %prepare.1 = (s32[9]{0:T(128)S(1)}, f32[6,32,4096]{2,1,0:T(8,128)S(1)}, bf16[256,256]{1,0:T(8,128)(2,1)S(1)}, f32[56,8,128]{2,1,0:T(8,128)S(1)}) custom-call(s32[1,4,2]{2,1,0:T(4,128)S(1)} %copy.7.pairs_ref, s32[1]{0:T(128)S(6)} %copy.9.count_ref, f32[2,32,4096]{2,1,0:T(8,128)S(1)} %copy-done, bf16[256,256]{1,0:T(8,128)(2,1)S(1)} %copy-done.2, ...), custom_call_target="tpu_custom_call" | custom-call | tf_op jit(solution)/shard_map/prepare/pallas_call | solution.py:378
  21.1 1.9 %collective-permute-start.1 = (f32[2,32,4096]{2,1,0:T(8,128)S(1)}, f32[2,32,4096]{2,1,0:T(8,128)S(1)}, u32[]{:S(2)}, u32[]{:S(2)}) collective-permute-start(f32[2,32,4096]{2,1,0:T(8,128)S(1)} %copy-done), channel_id=1, source_target_pairs={{0,2},{2,0},{4,6},{6,4},{8,10},{10,8},{12,14},{14,12},{16,18},{18,... | collective-permute-start | bytes 3145736 | tf_op jit(solution)/shard_map/ppermute | solution.py:439
  23.0 2.4 %collective-permute-start = (s32[9]{0:T(128)S(1)}, s32[9]{0:T(128)S(1)}, u32[]{:S(2)}, u32[]{:S(2)}) collective-permute-start(s32[9]{0:T(128)S(1)} %get-tuple-element.18), channel_id=1, source_target_pairs={{0,2},{2,4},{4,6},{6,8},{8,10},{10,12},{12,14},{14,16},{16,18},{18... | collective-permute-start | bytes 116 | tf_op jit(solution)/shard_map/ppermute | solution.py:439
  25.4 8.2 %collective-permute-done.ints_ref = s32[9]{0:T(128)S(1)} collective-permute-done((s32[9]{0:T(128)S(1)}, s32[9]{0:T(128)S(1)}, u32[]{:S(2)}, u32[]{:S(2)}) %collective-permute-start) | collective-permute-done | bytes 68 | tf_op jit(solution)/shard_map/ppermute | solution.py:439
  33.6 0.0 collective-permute-done.2.cross_ref
  33.6 0.0 collective-permute-done.1.mate_ref
  33.6 2.9 %forward.1 = (f32[4,4,32,8,128]{4,3,2,1,0:T(8,128)S(1)}, f32[4,2,4,8,128]{4,3,2,1,0:T(8,128)S(1)}, f32[6,32,4096]{2,1,0:T(8,128)S(1)}) custom-call(s32[9]{0:T(128)S(1)} %collective-permute-done.ints_ref, f32[2,32,4096]{2,1,0:T(8,128)S(1)} %collective-permute-done.1.mate_ref, ...), custom_call_target="tpu_custom_call", output_to_operand_aliasing={{2}: (3, {})} | custom-call | bytes 12000000 | tf_op jit(solution)/shard_map/forward/pallas_call | solution.py:396
  36.5 3.3 %collective-permute-start.3 = (f32[4,2,4,8,128]{4,3,2,1,0:T(8,128)S(1)}, f32[4,2,4,8,128]{4,3,2,1,0:T(8,128)S(1)}, u32[]{:S(2)}, u32[]{:S(2)}) collective-permute-start(f32[4,2,4,8,128]{4,3,2,1,0:T(8,128)S(1)} %get-tuple-element.25.edge_ref), channel_id=1, source_target_pairs={{0,1},{1,0},{2,3},{3,2},{4,5},{5,4},{6,7},{7,6},{8,9},{9,8},{10,11... | collective-permute-start | bytes 393224 | tf_op jit(solution)/shard_map/ppermute | solution.py:439
  39.8 3.5 %collective-permute-done.3.other_ref = f32[4,2,4,8,128]{4,3,2,1,0:T(8,128)S(1)} collective-permute-done((f32[4,2,4,8,128]{4,3,2,1,0:T(8,128)S(1)}, f32[4,2,4,8,128]{4,3,2,1,0:T(8,128)S(1)}, u32[]{:S(2)}, u32[]{:S(2)}) %collective-permute-start.3) | collective-permute-done | bytes 131104 | tf_op jit(solution)/shard_map/ppermute | solution.py:439
  43.3 4.1 %back.1 = (f32[2,32,4096]{2,1,0:T(8,128)S(1)}, f32[2,32,4096]{2,1,0:T(8,128)S(1)}, f32[2,32,4096]{2,1,0:T(8,128)S(1)}) custom-call(s32[9]{0:T(128)S(1)} %collective-permute-done.ints_ref, f32[6,32,4096]{2,1,0:T(8,128)S(1)} %get-tuple-element.23.window, f32[4,4,32,8,128]{4,3,2,1,0:T(8,128)S(1)} %get-tuple-element.24.local_ref, ...), custom_call_target="tpu_custom_call" | custom-call | bytes 12000000 | tf_op jit(solution)/shard_map/back/pallas_call | solution.py:420
  47.4 2.2 %collective-permute-start.4 = (f32[2,32,4096]{2,1,0:T(8,128)S(1)}, f32[2,32,4096]{2,1,0:T(8,128)S(1)}, u32[]{:S(2)}, u32[]{:S(2)}) collective-permute-start(f32[2,32,4096]{2,1,0:T(8,128)S(1)} %get-tuple-element.27), channel_id=1, source_target_pairs={{0,510},{2,4},{4,2},{6,8},{8,6},{10,12},{12,10},{14,16},{16,14},{1... | collective-permute-start | bytes 3145736 | tf_op jit(solution)/shard_map/ppermute | solution.py:439
  49.6 1.9 %collective-permute-start.5 = (f32[2,32,4096]{2,1,0:T(8,128)S(1)}, f32[2,32,4096]{2,1,0:T(8,128)S(1)}, u32[]{:S(2)}, u32[]{:S(2)}) collective-permute-start(f32[2,32,4096]{2,1,0:T(8,128)S(1)} %get-tuple-element.28), channel_id=1, source_target_pairs={{0,2},{2,0},{4,6},{6,4},{8,10},{10,8},{12,14},{14,12},{16,18},{18,... | collective-permute-start | bytes 3145736 | tf_op jit(solution)/shard_map/ppermute | solution.py:439
  51.5 17.7 %collective-permute-done.4 = f32[2,32,4096]{2,1,0:T(8,128)S(1)} collective-permute-done((f32[2,32,4096]{2,1,0:T(8,128)S(1)}, f32[2,32,4096]{2,1,0:T(8,128)S(1)}, u32[]{:S(2)}, u32[]{:S(2)}) %collective-permute-start.4) | collective-permute-done | bytes 1048608 | tf_op jit(solution)/shard_map/ppermute | solution.py:439
  69.3 0.0 collective-permute-done.5
  69.3 1.2 %add_add_fusion = f32[2,32,4096]{2,1,0:T(8,128)} fusion(f32[2,32,4096]{2,1,0:T(8,128)S(1)} %collective-permute-done.5, f32[2,32,4096]{2,1,0:T(8,128)S(1)} %get-tuple-element.26, f32[2,32,4096]{2,1,0:T(8,128)S(1)} %collective-permute-done.4), kind=kLoop, calls=%fused_computation | loop fusion | flops 524288 | bytes 4194304 | tf_op jit(solution)/shard_map/add | solution.py:463
Async XLA Ops:
  0.0 33.6 %collective-permute-start.2 = (f32[2,32,4096]{2,1,0:T(8,128)}, f32[2,32,4096]{2,1,0:T(8,128)S(1)}, u32[]{:S(2)}, u32[]{:S(2)}) collective-permute-start(f32[2,32,4096]{2,1,0:T(8,128)} %own_ref.1), channel_id=1, source_target_pairs={{0,510},{2,4},{4,2},{6,8},{8,6},{10,12},{12,10},{14,16},{16,14},{1... | collective-permute-start | bytes 3145736 | tf_op jit(solution)/shard_map/ppermute | solution.py:439
  16.3 1.2 %copy-start = (f32[2,32,4096]{2,1,0:T(8,128)S(1)}, f32[2,32,4096]{2,1,0:T(8,128)}, u32[]{:S(2)}) copy-start(f32[2,32,4096]{2,1,0:T(8,128)} %own_ref.1) | copy-start | bytes 3145732
  17.5 0.9 %copy-start.1 = (f32[56,8,128]{2,1,0:T(8,128)S(1)}, f32[56,8,128]{2,1,0:T(8,128)}, u32[]{:S(2)}) copy-start(f32[56,8,128]{2,1,0:T(8,128)} %constant.5.clone.table_ref) | copy-start | bytes 688132
  18.4 0.9 %copy-start.2 = (bf16[256,256]{1,0:T(8,128)(2,1)S(1)}, bf16[256,256]{1,0:T(8,128)(2,1)}, u32[]{:S(2)}) copy-start(bf16[256,256]{1,0:T(8,128)(2,1)} %constant.4.clone.weight_ref) | copy-start | bytes 393220
  21.1 12.5 %collective-permute-start.1 = (f32[2,32,4096]{2,1,0:T(8,128)S(1)}, f32[2,32,4096]{2,1,0:T(8,128)S(1)}, u32[]{:S(2)}, u32[]{:S(2)}) collective-permute-start(f32[2,32,4096]{2,1,0:T(8,128)S(1)} %copy-done), channel_id=1, source_target_pairs={{0,2},{2,0},{4,6},{6,4},{8,10},{10,8},{12,14},{14,12},{16,18},{18,... | collective-permute-start | bytes 3145736 | tf_op jit(solution)/shard_map/ppermute | solution.py:439
  23.0 10.6 %collective-permute-start = (s32[9]{0:T(128)S(1)}, s32[9]{0:T(128)S(1)}, u32[]{:S(2)}, u32[]{:S(2)}) collective-permute-start(s32[9]{0:T(128)S(1)} %get-tuple-element.18), channel_id=1, source_target_pairs={{0,2},{2,4},{4,6},{6,8},{8,10},{10,12},{12,14},{14,16},{16,18},{18... | collective-permute-start | bytes 116 | tf_op jit(solution)/shard_map/ppermute | solution.py:439
  36.5 6.9 %collective-permute-start.3 = (f32[4,2,4,8,128]{4,3,2,1,0:T(8,128)S(1)}, f32[4,2,4,8,128]{4,3,2,1,0:T(8,128)S(1)}, u32[]{:S(2)}, u32[]{:S(2)}) collective-permute-start(f32[4,2,4,8,128]{4,3,2,1,0:T(8,128)S(1)} %get-tuple-element.25.edge_ref), channel_id=1, source_target_pairs={{0,1},{1,0},{2,3},{3,2},{4,5},{5,4},{6,7},{7,6},{8,9},{9,8},{10,11... | collective-permute-start | bytes 393224 | tf_op jit(solution)/shard_map/ppermute | solution.py:439
  47.4 21.8 %collective-permute-start.4 = (f32[2,32,4096]{2,1,0:T(8,128)S(1)}, f32[2,32,4096]{2,1,0:T(8,128)S(1)}, u32[]{:S(2)}, u32[]{:S(2)}) collective-permute-start(f32[2,32,4096]{2,1,0:T(8,128)S(1)} %get-tuple-element.27), channel_id=1, source_target_pairs={{0,510},{2,4},{4,2},{6,8},{8,6},{10,12},{12,10},{14,16},{16,14},{1... | collective-permute-start | bytes 3145736 | tf_op jit(solution)/shard_map/ppermute | solution.py:439
  49.6 19.7 %collective-permute-start.5 = (f32[2,32,4096]{2,1,0:T(8,128)S(1)}, f32[2,32,4096]{2,1,0:T(8,128)S(1)}, u32[]{:S(2)}, u32[]{:S(2)}) collective-permute-start(f32[2,32,4096]{2,1,0:T(8,128)S(1)} %get-tuple-element.28), channel_id=1, source_target_pairs={{0,2},{2,0},{4,6},{6,4},{8,10},{10,8},{12,14},{14,12},{16,18},{18,... | collective-permute-start | bytes 3145736 | tf_op jit(solution)/shard_map/ppermute | solution.py:439

commit v2 on v1

--- a/solution.py
+++ b/solution.py
@@ -13,7 +13,6 @@
 SIDE = 64
 TILES = SIDE // 2
 LANES = 2 * SIDE
-BACK_CHUNKS = 1
 GROUPS = TILES // 8
 FACTORS = 36
 
@@ -158,8 +157,7 @@
     low = (matrix - high.astype(np.float64)).astype(ml_dtypes.bfloat16)
     row = np.concatenate([high, low], 1)
     weights = np.concatenate([row, row], 0)
-    rows = SIDE // 2 // BACK_CHUNKS
-    plain = np.stack([ratio, scale, ratio**rows, ratio**32, 1.0 / (1.0 - ratio**64)])
+    plain = np.stack([ratio, scale, ratio**32, 1.0 / (1.0 - ratio**64)])
     factors = np.repeat(FACTOR_ROWS[:, None, :], 8, 1)
     table = np.concatenate([factors, plain.reshape(-1, 8, LANES)], 0)
     return weights, table.astype(np.float32)
@@ -211,9 +209,16 @@
     return 4 * lax.rem(lax.axis_index("band"), 2)
 
 
+def pack_kernel(pairs_ref, count_ref, ints_ref):
+    for n in range(4):
+        ints_ref[2 * n] = pairs_ref[0, n, 0]
+        ints_ref[2 * n + 1] = pairs_ref[0, n, 1]
+    ints_ref[8] = count_ref[0]
+
+
 def prepare_kernel(
-    pairs_ref, count_ref, own_ref, weight_ref, table_ref,
-    ints_ref, window, weights, table, sems,
+    own_ref, weight_ref, table_ref,
+    window, result, weights, table, sems,
 ):
     copies = [
         pltpu.make_async_copy(own_ref, window.at[pl.ds(2, 2)], sems.at[0]),
@@ -222,34 +227,35 @@
     ]
     for copy in copies:
         copy.start()
-    for n in range(4):
-        ints_ref[2 * n] = pairs_ref[0, n, 0]
-        ints_ref[2 * n + 1] = pairs_ref[0, n, 1]
-    ints_ref[8] = count_ref[0]
+    result[...] = jnp.zeros_like(result)
     for copy in copies:
         copy.wait()
 
 
 def forward_kernel(
-    ints_ref, mate_ref, cross_ref, window_ref, weights, table,
+    ints_ref, cross_ref, mate_ref, window_ref, weights, table,
     local_ref, edge_ref, window,
     stage, sems,
 ):
     rows = window.shape[1]
     cross = cross_at()
-    copies = [
-        pltpu.make_async_copy(mate_ref, window.at[pl.ds(4 - cross, 2)], sems.at[0]),
-        pltpu.make_async_copy(cross_ref, window.at[pl.ds(cross, 2)], sems.at[1]),
-    ]
-    for copy in copies:
-        copy.start()
-    for copy in copies:
-        copy.wait()
+    copies = []
+    for o in range(rows // 8):
+        span = pl.ds(8 * o, 8)
+        copies.append([
+            pltpu.make_async_copy(ref.at[:, span], window.at[pl.ds(at, 2), span], sems.at[n, o])
+            for n, (ref, at) in enumerate(((mate_ref, 4 - cross), (cross_ref, cross)))
+        ])
+        for copy in copies[o]:
+            copy.start()
     factors = kernel_factors(table)
 
     def along_y(slot):
         first, second, alive = pair_rows(ints_ref, slot)
         for o in range(rows // 8):
+            if slot == 0:
+                for copy in copies[o]:
+                    copy.wait()
             values = []
             for t in range(TILES):
                 left = window[first, pl.ds(8 * o, 8), lanes_of(t)]
@@ -292,26 +298,18 @@
 
 
 def back_kernel(
-    rows, chunk,
-    ints_ref, window, local_ref, edge_ref, other_ref, weights, table, *rest,
+    ints_ref, window, local_ref, edge_ref, other_ref, weights, table, zero_ref,
+    cross_ref, mate_ref, own_ref, result,
+    fields, sems,
 ):
-    if chunk:
-        rest = rest[2:]
-    cross_ref, mate_ref, own_ref, result, fields, out_sems = rest
+    rows = window.shape[1]
     cross = cross_at()
-    begin = chunk * rows
-    result[...] = jnp.zeros_like(result)
     factors = kernel_factors(table)
 
     def along_xz(slot, g):
-        ratio, step = plain(table, 0, g), plain(table, 2, g)
-        whole, closing = plain(table, 3, g), plain(table, 4, g)
+        ratio, whole, closing = [plain(table, kind, g) for kind in (0, 2, 3)]
         ahead = (other_ref[slot, 0, g] + whole * edge_ref[slot, 0, g]) * closing
-        for _ in range(chunk):
-            ahead = ahead * step
         behind = (other_ref[slot, 1, g] + whole * edge_ref[slot, 1, g]) * closing
-        for _ in range(BACK_CHUNKS - 1 - chunk):
-            behind = behind * step
         behinds = []
         for x in range(rows):
             behind = behind * ratio
@@ -319,7 +317,7 @@
         parts = []
         for x in range(rows):
             ahead = ahead * ratio
-            parts.append(local_ref[slot, g, begin + x] + (ahead + behinds[rows - 1 - x]))
+            parts.append(local_ref[slot, g, x] + (ahead + behinds[rows - 1 - x]))
         values = transform_rows(jnp.concatenate(parts, 0), weights[...])
         for x in range(rows):
             fields[slot, pl.ds(x * TILES + 8 * g, 8)] = values[8 * x : 8 * x + 8]
@@ -331,36 +329,36 @@
                 fields[slot, pl.ds(8 * o * TILES + t, 8, stride=TILES)] for t in range(TILES)
             ]
             values = real_back(values, SIDE, factors)
-            here = pl.ds(8 * o, 8)
-            there = pl.ds(begin + 8 * o, 8)
+            span = pl.ds(8 * o, 8)
             for begin_t in range(0, TILES, 8):
                 new = []
                 for t in range(begin_t, begin_t + 8):
-                    left = window[first, there, lanes_of(t)]
-                    right = window[second, there, lanes_of(t)]
+                    left = window[first, span, lanes_of(t)]
+                    right = window[second, span, lanes_of(t)]
                     new.append((
-                        result[first, here, lanes_of(t)] + values[t] * right,
-                        result[second, here, lanes_of(t)] + values[t] * left,
+                        result[first, span, lanes_of(t)] + values[t] * right,
+                        result[second, span, lanes_of(t)] + values[t] * left,
                     ))
                 for t in range(begin_t, begin_t + 8):
-                    result[first, here, lanes_of(t)] = new[t - begin_t][0]
+                    result[first, span, lanes_of(t)] = new[t - begin_t][0]
                 for t in range(begin_t, begin_t + 8):
-                    result[second, here, lanes_of(t)] = new[t - begin_t][1]
-
+                    result[second, span, lanes_of(t)] = new[t - begin_t][1]
+            if slot == 3:
+                for n, (ref, at) in enumerate(
+                    ((cross_ref, cross), (mate_ref, 4 - cross), (own_ref, 2))
+                ):
+                    copies.append(pltpu.make_async_copy(
+                        result.at[pl.ds(at, 2), span], ref.at[:, span], sems.at[n, o]
+                    ))
+                    copies[-1].start()
+
+    copies = []
     for slot in range(5):
         if slot < 4:
             for g in range(GROUPS):
                 along_xz(slot, g)
         if slot:
             along_y(slot - 1)
-    span = pl.ds(begin, rows)
-    copies = [
-        pltpu.make_async_copy(result.at[pl.ds(cross, 2)], cross_ref, out_sems.at[0]),
-        pltpu.make_async_copy(result.at[pl.ds(4 - cross, 2)], mate_ref.at[:, span], out_sems.at[1]),
-        pltpu.make_async_copy(result.at[pl.ds(2, 2)], own_ref.at[:, span], out_sems.at[2]),
-    ]
-    for copy in copies:
-        copy.start()
     for copy in copies:
         copy.wait()
 
@@ -373,25 +371,36 @@
 COST = pl.CostEstimate(flops=0, bytes_accessed=12_000_000, transcendentals=0)
 
 
-def prepare(pair_list, pair_count, own):
-    rows = own.shape[1]
+def pack(pair_list, pair_count):
+    return pl.pallas_call(
+        pack_kernel,
+        out_shape=jax.ShapeDtypeStruct((9,), jnp.int32),
+        in_specs=[SMEM, SMEM],
+        out_specs=SMEM,
+        name="pack",
+    )(pair_list, pair_count)
+
+
+def prepare(own):
+    shape = (6,) + own.shape[1:]
     return pl.pallas_call(
         prepare_kernel,
         out_shape=(
-            jax.ShapeDtypeStruct((9,), jnp.int32),
-            jax.ShapeDtypeStruct((6, rows, SIDE * SIDE), jnp.float32),
+            jax.ShapeDtypeStruct(shape, jnp.float32),
+            jax.ShapeDtypeStruct(shape, jnp.float32),
             jax.ShapeDtypeStruct(WEIGHTS.shape, jnp.bfloat16),
             jax.ShapeDtypeStruct(TABLE.shape, jnp.float32),
         ),
-        in_specs=[SMEM, SMEM, HBM, HBM, HBM],
-        out_specs=(SMEM, VMEM, VMEM, VMEM),
+        in_specs=[HBM, HBM, HBM],
+        out_specs=(VMEM, VMEM, VMEM, VMEM),
         scratch_shapes=[pltpu.SemaphoreType.DMA((3,))],
         compiler_params=LIMIT,
+        cost_estimate=COST,
         name="prepare",
-    )(pair_list, pair_count, own, WEIGHTS, TABLE)
-
-
-def forward(ints, mate, cross, window, weights, table):
+    )(own, WEIGHTS, TABLE)
+
+
+def forward(ints, cross, mate, window, weights, table):
     rows = window.shape[1]
     return pl.pallas_call(
         forward_kernel,
@@ -405,33 +414,31 @@
         input_output_aliases={3: 2},
         scratch_shapes=[
             pltpu.VMEM((4, rows * TILES, LANES), jnp.float32),
-            pltpu.SemaphoreType.DMA((2,)),
+            pltpu.SemaphoreType.DMA((2, rows // 8)),
         ],
         compiler_params=LIMIT,
         cost_estimate=COST,
         name="forward",
-    )(ints, mate, cross, window, weights, table)
-
-
-def back(ints, window, local, edges, other, weights, table, chunk, carried):
-    rows = window.shape[1] // BACK_CHUNKS
-    part = jax.ShapeDtypeStruct((2, rows, SIDE * SIDE), jnp.float32)
-    block = jax.ShapeDtypeStruct((2, rows * BACK_CHUNKS, SIDE * SIDE), jnp.float32)
+    )(ints, cross, mate, window, weights, table)
+
+
+def back(ints, window, local, edges, other, weights, table, result):
+    rows = window.shape[1]
+    block = jax.ShapeDtypeStruct((2, rows, SIDE * SIDE), jnp.float32)
     return pl.pallas_call(
-        functools.partial(back_kernel, rows, chunk),
-        out_shape=(part, block, block),
-        in_specs=[SMEM] + [VMEM] * 6 + [ANY] * len(carried),
-        out_specs=(ANY, ANY, ANY),
-        input_output_aliases={7: 1, 8: 2} if carried else {},
+        back_kernel,
+        out_shape=(block, block, block, jax.ShapeDtypeStruct(result.shape, jnp.float32)),
+        in_specs=[SMEM] + [VMEM] * 7,
+        out_specs=(ANY, ANY, ANY, VMEM),
+        input_output_aliases={7: 3},
         scratch_shapes=[
-            pltpu.VMEM((6, rows, SIDE * SIDE), jnp.float32),
             pltpu.VMEM((4, rows * TILES, LANES), jnp.float32),
-            pltpu.SemaphoreType.DMA((3,)),
+            pltpu.SemaphoreType.DMA((3, rows // 8)),
         ],
         compiler_params=LIMIT,
         cost_estimate=COST,
         name="back",
-    )(ints, window, local, edges, other, weights, table, *carried)
+    )(ints, window, local, edges, other, weights, table, result)
 
 
 def moved(value, axis, target):
@@ -447,20 +454,21 @@
     return moved(value, "band", lambda n: n + 1 if n % 2 else n - 1)
 
 
+def to_next_other_slab(value):
+    count = lax.axis_size("band")
+    pairs = [(2 * n + g, 2 * ((n + 1) % count) + 1 - g) for n in range(count) for g in range(2)]
+    return lax.ppermute(value, ("band", "grid"), pairs)
+
+
 def on_device(orbitals, pair_list, pair_count):
     cross = to_cross(orbitals)
-    ints, window, weights, table = prepare(pair_list, pair_count, orbitals)
-    held, ints = lax.optimization_barrier((orbitals, ints))
-    ints = moved(ints, "band", lambda n: n + 1)
-    mate = to_mate(held)
-    local, edges, window = forward(ints, mate, cross, window, weights, table)
+    mate = to_mate(orbitals)
+    ints = to_next_other_slab(pack(pair_list, pair_count))
+    window, result, weights, table = prepare(orbitals)
+    local, edges, window = forward(ints, cross, mate, window, weights, table)
     other = moved(edges, "grid", lambda n: n + 1)
-    returned, carried = [], ()
-    for chunk in range(BACK_CHUNKS):
-        part, *carried = back(ints, window, local, edges, other, weights, table, chunk, carried)
-        returned.append(to_cross(part))
-    mate, own = carried
-    return (own + returned[0]) + to_mate(mate)
+    cross, mate, own, _ = back(ints, window, local, edges, other, weights, table, result)
+    return (own + to_cross(cross)) + to_mate(mate)
 
 
 def solution(mesh):

time: 70.8 us -> 67 us (0.946)
  waiting for transfers between devices: 29.4 us -> 19 us
  starting transfers between devices: 26.6 us -> 32.5 us
    ppermute x6 -> x5, waiting for transfers between devices: 29.4 us -> 17 us  [moved(): lax.ppermute(value, axis, [(n, target(n) % count) for n in range(count)])]
    ppermute x0 -> x1, starting transfers between devices: none -> 3.44 us  [to_next_other_slab(): return lax.ppermute(value, ('band', 'grid'), pairs)]
    ppermute x6 -> x5, starting transfers between devices: 26.6 us -> 29.1 us  [moved(): lax.ppermute(value, axis, [(n, target(n) % count) for n in range(count)])]
    ppermute x0 -> x1, waiting for transfers between devices: none -> 2.02 us  [to_next_other_slab(): return lax.ppermute(value, ('band', 'grid'), pairs)]
    pallas_call x2 -> x3, Pallas kernels: 5.81 us -> 5.91 us  [the longest x1 3.96 us: back(): pl.pallas_call(back_kernel, out_shape=(block, block, block, jax.ShapeDtyp...]
  transfers between devices with their start and end apart: 6 -> 6, of which waited for: 3 -> 3; matrix products, arithmetic and copies ran while one was open for 1% -> 2% of each run, Pallas kernels for 2% -> 3%
where the time goes in v2:
time: 67 us; the launch traced here: 66.7 us
  starting transfers between devices  32.5 us (49%)
  waiting for transfers between devices  19 us (28%)
  Pallas kernels  8.85 us (13%)
  local copies, waits for them, and re-layouts  4.39 us (7%)
  other arithmetic  1.12 us (2%)
  between operations  0.74 us (1%)
    ppermute x5, starting transfers between devices, moved(): lax.ppermute(value, axis, [(n, target(n) % count) for n in range(count)])  29.1 us
    ppermute x5, waiting for transfers between devices, moved(): lax.ppermute(value, axis, [(n, target(n) % count) for n in range(count)])  17 us
    unnamed x7, local copies, waits for them, and re-layouts  4.39 us
    pallas_call x1, Pallas kernels, back(): pl.pallas_call(back_kernel, out_shape=(block, block, block, jax.ShapeDtyp...  3.96 us
    ppermute x1, starting transfers between devices, to_next_other_slab(): return lax.ppermute(value, ('band', 'grid'), pairs)  3.44 us
    pallas_call x1, Pallas kernels, forward(): pl.pallas_call(forward_kernel, out_shape=(jax.ShapeDtypeStruct((4, GROUPS...  2.94 us
    ppermute x1, waiting for transfers between devices, to_next_other_slab(): return lax.ppermute(value, ('band', 'grid'), pairs)  2.02 us
  transfers between devices with their start and end apart: 6, of which 3 were waited for; matrix products, arithmetic and copies ran while one was open for 2% of the time, Pallas kernels for 3%

profile of v2, /device:TPU:2, one launch (start us, length us, event | category | flops | bytes accessed | tf_op | source)
XLA Modules:
  0.0 66.7 jit_solution(7872448706078559262)
XLA Ops:
  0.0 14.8 %collective-permute-start.1 = (f32[2,32,4096]{2,1,0:T(8,128)}, f32[2,32,4096]{2,1,0:T(8,128)S(1)}, u32[]{:S(2)}, u32[]{:S(2)}) collective-permute-start(f32[2,32,4096]{2,1,0:T(8,128)} %own_ref.1), channel_id=1, source_target_pairs={{0,510},{2,4},{4,2},{6,8},{8,6},{10,12},{12,10},{14,16},{16,14},{1... | collective-permute-start | bytes 3145736 | tf_op jit(solution)/shard_map/ppermute | solution.py:446
  14.9 1.9 %collective-permute-start.2 = (f32[2,32,4096]{2,1,0:T(8,128)}, f32[2,32,4096]{2,1,0:T(8,128)S(1)}, u32[]{:S(2)}, u32[]{:S(2)}) collective-permute-start(f32[2,32,4096]{2,1,0:T(8,128)} %own_ref.1), channel_id=1, source_target_pairs={{0,2},{2,0},{4,6},{6,4},{8,10},{10,8},{12,14},{14,12},{16,18},{18,... | collective-permute-start | bytes 3145736 | tf_op jit(solution)/shard_map/ppermute | solution.py:446
  17.4 1.3 %copy.8.pairs_ref = s32[1,4,2]{2,1,0:T(4,128)} copy(s32[1,4,2]{1,2,0:T(2,128)} %param.6) | data formatting | bytes 64 | tf_op args[1]
  18.8 1.2 %pack.1 = s32[9]{0:T(128)} custom-call(s32[1,4,2]{2,1,0:T(4,128)} %copy.8.pairs_ref, s32[1]{0:T(128)S(6)} %copy.11.count_ref), custom_call_target="tpu_custom_call" | custom-call | tf_op jit(solution)/shard_map/pack/pallas_call | solution.py:375
  20.0 3.4 %collective-permute-start = (s32[9]{0:T(128)}, s32[9]{0:T(128)S(1)}, u32[]{:S(2)}, u32[]{:S(2)}) collective-permute-start(s32[9]{0:T(128)} %pack.1), channel_id=1, source_target_pairs={{0,3},{1,2},{2,5},{3,4},{4,7},{5,6},{6,9},{7,8},{8,11},{9,10},{10,... | collective-permute-start | bytes 116 | tf_op jit(solution)/shard_map/ppermute | solution.py:460
  23.4 0.0 copy-start
  23.4 1.2 %copy-done = f32[2,32,4096]{2,1,0:T(8,128)S(1)} copy-done((f32[2,32,4096]{2,1,0:T(8,128)S(1)}, f32[2,32,4096]{2,1,0:T(8,128)}, u32[]{:S(2)}) %copy-start) | copy-done | bytes 1048600
  24.7 0.0 copy-start.1
  24.7 0.9 %copy-done.1 = f32[52,8,128]{2,1,0:T(8,128)S(1)} copy-done((f32[52,8,128]{2,1,0:T(8,128)S(1)}, f32[52,8,128]{2,1,0:T(8,128)}, u32[]{:S(2)}) %copy-start.1) | copy-done | bytes 213016
  25.6 0.0 copy-start.2
  25.6 0.9 %copy-done.2 = bf16[256,256]{1,0:T(8,128)(2,1)S(1)} copy-done((bf16[256,256]{1,0:T(8,128)(2,1)S(1)}, bf16[256,256]{1,0:T(8,128)(2,1)}, u32[]{:S(2)}) %copy-start.2) | copy-done | bytes 131096
  26.5 0.7 %prepare.1 = (f32[6,32,4096]{2,1,0:T(8,128)S(1)}, f32[6,32,4096]{2,1,0:T(8,128)S(1)}, bf16[256,256]{1,0:T(8,128)(2,1)S(1)}, f32[52,8,128]{2,1,0:T(8,128)S(1)}) custom-call(f32[2,32,4096]{2,1,0:T(8,128)S(1)} %copy-done, bf16[256,256]{1,0:T(8,128)(2,1)S(1)} %copy-done.2, f32[52,8,128]{2,1,0:T(8,128)S(1)} %copy-done.1), custom_call_target="tpu_custom_call" | custom-call | bytes 12000000 | tf_op jit(solution)/shard_map/prepare/pallas_call | solution.py:386
  27.3 2.0 %collective-permute-done.ints_ref = s32[9]{0:T(128)S(1)} collective-permute-done((s32[9]{0:T(128)}, s32[9]{0:T(128)S(1)}, u32[]{:S(2)}, u32[]{:S(2)}) %collective-permute-start) | collective-permute-done | bytes 68 | tf_op jit(solution)/shard_map/ppermute | solution.py:460
  29.3 0.0 collective-permute-done.1.cross_ref
  29.3 0.0 collective-permute-done.2.mate_ref
  29.3 2.9 %forward.1 = (f32[4,4,32,8,128]{4,3,2,1,0:T(8,128)S(1)}, f32[4,2,4,8,128]{4,3,2,1,0:T(8,128)S(1)}, f32[6,32,4096]{2,1,0:T(8,128)S(1)}) custom-call(s32[9]{0:T(128)S(1)} %collective-permute-done.ints_ref, f32[2,32,4096]{2,1,0:T(8,128)S(1)} %collective-permute-done.1.cross_ref, ...), custom_call_target="tpu_custom_call", output_to_operand_aliasing={{2}: (3, {})} | custom-call | bytes 12000000 | tf_op jit(solution)/shard_map/forward/pallas_call | solution.py:405
  32.2 4.6 %collective-permute-start.3 = (f32[4,2,4,8,128]{4,3,2,1,0:T(8,128)S(1)}, f32[4,2,4,8,128]{4,3,2,1,0:T(8,128)S(1)}, u32[]{:S(2)}, u32[]{:S(2)}) collective-permute-start(f32[4,2,4,8,128]{4,3,2,1,0:T(8,128)S(1)} %get-tuple-element.20.edge_ref), channel_id=1, source_target_pairs={{0,1},{1,0},{2,3},{3,2},{4,5},{5,4},{6,7},{7,6},{8,9},{9,8},{10,11... | collective-permute-start | bytes 393224 | tf_op jit(solution)/shard_map/ppermute | solution.py:446
  36.8 2.9 %collective-permute-done.3.other_ref = f32[4,2,4,8,128]{4,3,2,1,0:T(8,128)S(1)} collective-permute-done((f32[4,2,4,8,128]{4,3,2,1,0:T(8,128)S(1)}, f32[4,2,4,8,128]{4,3,2,1,0:T(8,128)S(1)}, u32[]{:S(2)}, u32[]{:S(2)}) %collective-permute-start.3) | collective-permute-done | bytes 131104 | tf_op jit(solution)/shard_map/ppermute | solution.py:446
  39.7 4.0 %back.1 = (f32[2,32,4096]{2,1,0:T(8,128)S(1)}, f32[2,32,4096]{2,1,0:T(8,128)S(1)}, f32[2,32,4096]{2,1,0:T(8,128)S(1)}, f32[6,32,4096]{2,1,0:T(8,128)S(1)}) custom-call(s32[9]{0:T(128)S(1)} %collective-permute-done.ints_ref, f32[6,32,4096]{2,1,0:T(8,128)S(1)} %get-tuple-element.18.window, ...), custom_call_target="tpu_custom_call", output_to_operand_aliasing={{3}: (7, {})} | custom-call | bytes 12000000 | tf_op jit(solution)/shard_map/back/pallas_call | solution.py:428
  43.7 5.8 %collective-permute-start.4 = (f32[2,32,4096]{2,1,0:T(8,128)S(1)}, f32[2,32,4096]{2,1,0:T(8,128)S(1)}, u32[]{:S(2)}, u32[]{:S(2)}) collective-permute-start(f32[2,32,4096]{2,1,0:T(8,128)S(1)} %get-tuple-element.23), channel_id=1, source_target_pairs={{0,510},{2,4},{4,2},{6,8},{8,6},{10,12},{12,10},{14,16},{16,14},{1... | collective-permute-start | bytes 3145736 | tf_op jit(solution)/shard_map/ppermute | solution.py:446
  49.5 1.9 %collective-permute-start.5 = (f32[2,32,4096]{2,1,0:T(8,128)S(1)}, f32[2,32,4096]{2,1,0:T(8,128)S(1)}, u32[]{:S(2)}, u32[]{:S(2)}) collective-permute-start(f32[2,32,4096]{2,1,0:T(8,128)S(1)} %get-tuple-element.24), channel_id=1, source_target_pairs={{0,2},{2,0},{4,6},{6,4},{8,10},{10,8},{12,14},{14,12},{16,18},{18,... | collective-permute-start | bytes 3145736 | tf_op jit(solution)/shard_map/ppermute | solution.py:446
  51.5 14.1 %collective-permute-done.4 = f32[2,32,4096]{2,1,0:T(8,128)S(1)} collective-permute-done((f32[2,32,4096]{2,1,0:T(8,128)S(1)}, f32[2,32,4096]{2,1,0:T(8,128)S(1)}, u32[]{:S(2)}, u32[]{:S(2)}) %collective-permute-start.4) | collective-permute-done | bytes 1048608 | tf_op jit(solution)/shard_map/ppermute | solution.py:446
  65.5 0.0 collective-permute-done.5
  65.5 1.1 %add_add_fusion = f32[2,32,4096]{2,1,0:T(8,128)} fusion(f32[2,32,4096]{2,1,0:T(8,128)S(1)} %collective-permute-done.5, f32[2,32,4096]{2,1,0:T(8,128)S(1)} %get-tuple-element.22, f32[2,32,4096]{2,1,0:T(8,128)S(1)} %collective-permute-done.4), kind=kLoop, calls=%fused_computation | loop fusion | flops 524288 | bytes 4194304 | tf_op jit(solution)/shard_map/add | solution.py:471
Async XLA Ops:
  0.0 29.3 %collective-permute-start.1 = (f32[2,32,4096]{2,1,0:T(8,128)}, f32[2,32,4096]{2,1,0:T(8,128)S(1)}, u32[]{:S(2)}, u32[]{:S(2)}) collective-permute-start(f32[2,32,4096]{2,1,0:T(8,128)} %own_ref.1), channel_id=1, source_target_pairs={{0,510},{2,4},{4,2},{6,8},{8,6},{10,12},{12,10},{14,16},{16,14},{1... | collective-permute-start | bytes 3145736 | tf_op jit(solution)/shard_map/ppermute | solution.py:446
  14.9 14.4 %collective-permute-start.2 = (f32[2,32,4096]{2,1,0:T(8,128)}, f32[2,32,4096]{2,1,0:T(8,128)S(1)}, u32[]{:S(2)}, u32[]{:S(2)}) collective-permute-start(f32[2,32,4096]{2,1,0:T(8,128)} %own_ref.1), channel_id=1, source_target_pairs={{0,2},{2,0},{4,6},{6,4},{8,10},{10,8},{12,14},{14,12},{16,18},{18,... | collective-permute-start | bytes 3145736 | tf_op jit(solution)/shard_map/ppermute | solution.py:446
  20.0 9.3 %collective-permute-start = (s32[9]{0:T(128)}, s32[9]{0:T(128)S(1)}, u32[]{:S(2)}, u32[]{:S(2)}) collective-permute-start(s32[9]{0:T(128)} %pack.1), channel_id=1, source_target_pairs={{0,3},{1,2},{2,5},{3,4},{4,7},{5,6},{6,9},{7,8},{8,11},{9,10},{10,... | collective-permute-start | bytes 116 | tf_op jit(solution)/shard_map/ppermute | solution.py:460
  23.4 1.2 %copy-start = (f32[2,32,4096]{2,1,0:T(8,128)S(1)}, f32[2,32,4096]{2,1,0:T(8,128)}, u32[]{:S(2)}) copy-start(f32[2,32,4096]{2,1,0:T(8,128)} %own_ref.1) | copy-start | bytes 3145732
  24.7 0.9 %copy-start.1 = (f32[52,8,128]{2,1,0:T(8,128)S(1)}, f32[52,8,128]{2,1,0:T(8,128)}, u32[]{:S(2)}) copy-start(f32[52,8,128]{2,1,0:T(8,128)} %constant.5.clone.table_ref) | copy-start | bytes 638980
  25.6 0.9 %copy-start.2 = (bf16[256,256]{1,0:T(8,128)(2,1)S(1)}, bf16[256,256]{1,0:T(8,128)(2,1)}, u32[]{:S(2)}) copy-start(bf16[256,256]{1,0:T(8,128)(2,1)} %constant.4.clone.weight_ref) | copy-start | bytes 393220
  32.2 7.5 %collective-permute-start.3 = (f32[4,2,4,8,128]{4,3,2,1,0:T(8,128)S(1)}, f32[4,2,4,8,128]{4,3,2,1,0:T(8,128)S(1)}, u32[]{:S(2)}, u32[]{:S(2)}) collective-permute-start(f32[4,2,4,8,128]{4,3,2,1,0:T(8,128)S(1)} %get-tuple-element.20.edge_ref), channel_id=1, source_target_pairs={{0,1},{1,0},{2,3},{3,2},{4,5},{5,4},{6,7},{7,6},{8,9},{9,8},{10,11... | collective-permute-start | bytes 393224 | tf_op jit(solution)/shard_map/ppermute | solution.py:446
  43.7 21.8 %collective-permute-start.4 = (f32[2,32,4096]{2,1,0:T(8,128)S(1)}, f32[2,32,4096]{2,1,0:T(8,128)S(1)}, u32[]{:S(2)}, u32[]{:S(2)}) collective-permute-start(f32[2,32,4096]{2,1,0:T(8,128)S(1)} %get-tuple-element.23), channel_id=1, source_target_pairs={{0,510},{2,4},{4,2},{6,8},{8,6},{10,12},{12,10},{14,16},{16,14},{1... | collective-permute-start | bytes 3145736 | tf_op jit(solution)/shard_map/ppermute | solution.py:446
  49.5 16.0 %collective-permute-start.5 = (f32[2,32,4096]{2,1,0:T(8,128)S(1)}, f32[2,32,4096]{2,1,0:T(8,128)S(1)}, u32[]{:S(2)}, u32[]{:S(2)}) collective-permute-start(f32[2,32,4096]{2,1,0:T(8,128)S(1)} %get-tuple-element.24), channel_id=1, source_target_pairs={{0,2},{2,0},{4,6},{6,4},{8,10},{10,8},{12,14},{14,12},{16,18},{18,... | collective-permute-start | bytes 3145736 | tf_op jit(solution)/shard_map/ppermute | solution.py:446

commit v3 on v2

--- a/solution.py
+++ b/solution.py
@@ -205,6 +205,16 @@
     return jnp.where(alive, first, 0), jnp.where(alive, second, 0), alive
 
 
+def for_slots(ints_ref, run):
+    band = lax.axis_index("band")
+    ends = (band == 0) | (band == lax.axis_size("band") - 1)
+    count = jnp.where(ends, ints_ref[8], 4)
+    pl.when(count == 1)(lambda: run((0,)))
+    pl.when((count == 2) | (count == 3))(lambda: run((0, 1)))
+    pl.when(count == 3)(lambda: run((2,)))
+    pl.when(count >= 4)(lambda: run((0, 1, 2, 3)))
+
+
 def cross_at():
     return 4 * lax.rem(lax.axis_index("band"), 2)
 
@@ -248,14 +258,14 @@
         ])
         for copy in copies[o]:
             copy.start()
+    for pair in copies:
+        for copy in pair:
+            copy.wait()
     factors = kernel_factors(table)
 
     def along_y(slot):
-        first, second, alive = pair_rows(ints_ref, slot)
+        first, second, _ = pair_rows(ints_ref, slot)
         for o in range(rows // 8):
-            if slot == 0:
-                for copy in copies[o]:
-                    copy.wait()
             values = []
             for t in range(TILES):
                 left = window[first, pl.ds(8 * o, 8), lanes_of(t)]
@@ -266,13 +276,12 @@
                 stage[slot, pl.ds((o * TILES + t) * 8, 8)] = values[t]
 
     def along_zx(slot, g):
-        alive = pair_rows(ints_ref, slot)[2]
-        weight = jnp.where(alive, 1.0, 0.0).astype(jnp.float32)
         parts = [
             stage[slot, pl.ds(x // 8 * TILES * 8 + g * 64 + x % 8, 8, stride=8)]
             for x in range(rows)
         ]
         spectrum = transform_rows(jnp.concatenate(parts, 0), weights[...])
+        weight = jnp.where(pair_rows(ints_ref, slot)[2], 1.0, 0.0).astype(jnp.float32)
         ratio, scale = plain(table, 0, g), plain(table, 1, g) * weight
         values = [spectrum[8 * x : 8 * x + 8] * scale for x in range(rows)]
         ahead = values[0]
@@ -289,12 +298,15 @@
         edge_ref[slot, 0, g] = ahead
         edge_ref[slot, 1, g] = behind
 
-    along_y(0)
-    for slot in range(4):
-        if slot < 3:
-            along_y(slot + 1)
-        for g in range(GROUPS):
-            along_zx(slot, g)
+    def run(slots):
+        along_y(slots[0])
+        for slot in slots:
+            if slot != slots[-1]:
+                along_y(slot + 1)
+            for g in range(GROUPS):
+                along_zx(slot, g)
+
+    for_slots(ints_ref, run)
 
 
 def back_kernel(
@@ -323,7 +335,7 @@
             fields[slot, pl.ds(x * TILES + 8 * g, 8)] = values[8 * x : 8 * x + 8]
 
     def along_y(slot):
-        first, second, alive = pair_rows(ints_ref, slot)
+        first, second, _ = pair_rows(ints_ref, slot)
         for o in range(rows // 8):
             values = [
                 fields[slot, pl.ds(8 * o * TILES + t, 8, stride=TILES)] for t in range(TILES)
@@ -343,22 +355,23 @@
                     result[first, span, lanes_of(t)] = new[t - begin_t][0]
                 for t in range(begin_t, begin_t + 8):
                     result[second, span, lanes_of(t)] = new[t - begin_t][1]
-            if slot == 3:
-                for n, (ref, at) in enumerate(
-                    ((cross_ref, cross), (mate_ref, 4 - cross), (own_ref, 2))
-                ):
-                    copies.append(pltpu.make_async_copy(
-                        result.at[pl.ds(at, 2), span], ref.at[:, span], sems.at[n, o]
-                    ))
-                    copies[-1].start()
-
-    copies = []
-    for slot in range(5):
-        if slot < 4:
-            for g in range(GROUPS):
-                along_xz(slot, g)
-        if slot:
-            along_y(slot - 1)
+
+    def run(slots):
+        for g in range(GROUPS):
+            along_xz(slots[0], g)
+        for slot in slots:
+            if slot != slots[-1]:
+                for g in range(GROUPS):
+                    along_xz(slot + 1, g)
+            along_y(slot)
+
+    for_slots(ints_ref, run)
+    copies = [
+        pltpu.make_async_copy(result.at[pl.ds(at, 2)], ref, sems.at[n])
+        for n, (ref, at) in enumerate(((cross_ref, cross), (mate_ref, 4 - cross), (own_ref, 2)))
+    ]
+    for copy in copies:
+        copy.start()
     for copy in copies:
         copy.wait()
 
@@ -433,7 +446,7 @@
         input_output_aliases={7: 3},
         scratch_shapes=[
             pltpu.VMEM((4, rows * TILES, LANES), jnp.float32),
-            pltpu.SemaphoreType.DMA((3, rows // 8)),
+            pltpu.SemaphoreType.DMA((3,)),
         ],
         compiler_params=LIMIT,
         cost_estimate=COST,

time: 67 us -> 65 us (0.970); the launches traced: 66.7 us -> 64 us
  Pallas kernels: 8.85 us -> 6.18 us
  starting transfers between devices: 32.5 us -> 33.9 us
  waiting for transfers between devices: 19 us -> 17.7 us
    pallas_call x1, Pallas kernels: 3.96 us -> 2.35 us  [back(): pl.pallas_call(back_kernel, out_shape=(block, block, block, jax.ShapeDtyp...]
    ppermute x5, waiting for transfers between devices: 17 us -> 15.6 us  [moved(): lax.ppermute(value, axis, [(n, target(n) % count) for n in range(count)])]
    ppermute x5, starting transfers between devices: 29.1 us -> 30.5 us  [moved(): lax.ppermute(value, axis, [(n, target(n) % count) for n in range(count)])]
    pallas_call x1, Pallas kernels: 2.94 us -> 1.88 us  [forward(): pl.pallas_call(forward_kernel, out_shape=(jax.ShapeDtypeStruct((4, GROUPS...]
where the time goes in v3:
time: 65 us; the launch traced here: 64 us
  starting transfers between devices  33.9 us (52%)
  waiting for transfers between devices  17.7 us (27%)
  Pallas kernels  6.18 us (10%)
  local copies, waits for them, and re-layouts  4.39 us (7%)
  other arithmetic  1.12 us (2%)
  between operations  0.74 us (1%)
    ppermute x5, starting transfers between devices, moved(): lax.ppermute(value, axis, [(n, target(n) % count) for n in range(count)])  30.5 us
    ppermute x5, waiting for transfers between devices, moved(): lax.ppermute(value, axis, [(n, target(n) % count) for n in range(count)])  15.6 us
    unnamed x7, local copies, waits for them, and re-layouts  4.39 us
    ppermute x1, starting transfers between devices, to_next_other_slab(): return lax.ppermute(value, ('band', 'grid'), pairs)  3.44 us
    pallas_call x1, Pallas kernels, back(): pl.pallas_call(back_kernel, out_shape=(block, block, block, jax.ShapeDtyp...  2.35 us
    ppermute x1, waiting for transfers between devices, to_next_other_slab(): return lax.ppermute(value, ('band', 'grid'), pairs)  2.02 us
    pallas_call x1, Pallas kernels, forward(): pl.pallas_call(forward_kernel, out_shape=(jax.ShapeDtypeStruct((4, GROUPS...  1.88 us
  transfers between devices with their start and end apart: 6, of which 3 were waited for; matrix products, arithmetic and copies ran while one was open for 2% of the time, Pallas kernels for 3%

profile of v3, /device:TPU:2, one launch (start us, length us, event | category | flops | bytes accessed | tf_op | source)
XLA Modules:
  0.0 64.0 jit_solution(13011797977176718732)
XLA Ops:
  0.0 14.8 %collective-permute-start.1 = (f32[2,32,4096]{2,1,0:T(8,128)}, f32[2,32,4096]{2,1,0:T(8,128)S(1)}, u32[]{:S(2)}, u32[]{:S(2)}) collective-permute-start(f32[2,32,4096]{2,1,0:T(8,128)} %own_ref.1), channel_id=1, source_target_pairs={{0,510},{2,4},{4,2},{6,8},{8,6},{10,12},{12,10},{14,16},{16,14},{1... | collective-permute-start | bytes 3145736 | tf_op jit(solution)/shard_map/ppermute | solution.py:459
  14.9 1.9 %collective-permute-start.2 = (f32[2,32,4096]{2,1,0:T(8,128)}, f32[2,32,4096]{2,1,0:T(8,128)S(1)}, u32[]{:S(2)}, u32[]{:S(2)}) collective-permute-start(f32[2,32,4096]{2,1,0:T(8,128)} %own_ref.1), channel_id=1, source_target_pairs={{0,2},{2,0},{4,6},{6,4},{8,10},{10,8},{12,14},{14,12},{16,18},{18,... | collective-permute-start | bytes 3145736 | tf_op jit(solution)/shard_map/ppermute | solution.py:459
  17.4 1.3 %copy.8.pairs_ref = s32[1,4,2]{2,1,0:T(4,128)} copy(s32[1,4,2]{1,2,0:T(2,128)} %param.6) | data formatting | bytes 64 | tf_op args[1]
  18.8 1.2 %pack.1 = s32[9]{0:T(128)} custom-call(s32[1,4,2]{2,1,0:T(4,128)} %copy.8.pairs_ref, s32[1]{0:T(128)S(6)} %copy.11.count_ref), custom_call_target="tpu_custom_call" | custom-call | tf_op jit(solution)/shard_map/pack/pallas_call | solution.py:388
  20.0 3.4 %collective-permute-start = (s32[9]{0:T(128)}, s32[9]{0:T(128)S(1)}, u32[]{:S(2)}, u32[]{:S(2)}) collective-permute-start(s32[9]{0:T(128)} %pack.1), channel_id=1, source_target_pairs={{0,3},{1,2},{2,5},{3,4},{4,7},{5,6},{6,9},{7,8},{8,11},{9,10},{10,... | collective-permute-start | bytes 116 | tf_op jit(solution)/shard_map/ppermute | solution.py:473
  23.4 0.0 copy-start
  23.4 1.2 %copy-done = f32[2,32,4096]{2,1,0:T(8,128)S(1)} copy-done((f32[2,32,4096]{2,1,0:T(8,128)S(1)}, f32[2,32,4096]{2,1,0:T(8,128)}, u32[]{:S(2)}) %copy-start) | copy-done | bytes 1048600
  24.7 0.0 copy-start.1
  24.7 0.9 %copy-done.1 = f32[52,8,128]{2,1,0:T(8,128)S(1)} copy-done((f32[52,8,128]{2,1,0:T(8,128)S(1)}, f32[52,8,128]{2,1,0:T(8,128)}, u32[]{:S(2)}) %copy-start.1) | copy-done | bytes 213016
  25.6 0.0 copy-start.2
  25.6 0.9 %copy-done.2 = bf16[256,256]{1,0:T(8,128)(2,1)S(1)} copy-done((bf16[256,256]{1,0:T(8,128)(2,1)S(1)}, bf16[256,256]{1,0:T(8,128)(2,1)}, u32[]{:S(2)}) %copy-start.2) | copy-done | bytes 131096
  26.5 0.7 %prepare.1 = (f32[6,32,4096]{2,1,0:T(8,128)S(1)}, f32[6,32,4096]{2,1,0:T(8,128)S(1)}, bf16[256,256]{1,0:T(8,128)(2,1)S(1)}, f32[52,8,128]{2,1,0:T(8,128)S(1)}) custom-call(f32[2,32,4096]{2,1,0:T(8,128)S(1)} %copy-done, bf16[256,256]{1,0:T(8,128)(2,1)S(1)} %copy-done.2, f32[52,8,128]{2,1,0:T(8,128)S(1)} %copy-done.1), custom_call_target="tpu_custom_call" | custom-call | bytes 12000000 | tf_op jit(solution)/shard_map/prepare/pallas_call | solution.py:399
  27.3 2.0 %collective-permute-done.ints_ref = s32[9]{0:T(128)S(1)} collective-permute-done((s32[9]{0:T(128)}, s32[9]{0:T(128)S(1)}, u32[]{:S(2)}, u32[]{:S(2)}) %collective-permute-start) | collective-permute-done | bytes 68 | tf_op jit(solution)/shard_map/ppermute | solution.py:473
  29.3 0.0 collective-permute-done.1.cross_ref
  29.3 0.0 collective-permute-done.2.mate_ref
  29.3 1.9 %forward.1 = (f32[4,4,32,8,128]{4,3,2,1,0:T(8,128)S(1)}, f32[4,2,4,8,128]{4,3,2,1,0:T(8,128)S(1)}, f32[6,32,4096]{2,1,0:T(8,128)S(1)}) custom-call(s32[9]{0:T(128)S(1)} %collective-permute-done.ints_ref, f32[2,32,4096]{2,1,0:T(8,128)S(1)} %collective-permute-done.1.cross_ref, ...), custom_call_target="tpu_custom_call", output_to_operand_aliasing={{2}: (3, {})} | custom-call | bytes 12000000 | tf_op jit(solution)/shard_map/forward/pallas_call | solution.py:418
  31.2 4.6 %collective-permute-start.3 = (f32[4,2,4,8,128]{4,3,2,1,0:T(8,128)S(1)}, f32[4,2,4,8,128]{4,3,2,1,0:T(8,128)S(1)}, u32[]{:S(2)}, u32[]{:S(2)}) collective-permute-start(f32[4,2,4,8,128]{4,3,2,1,0:T(8,128)S(1)} %get-tuple-element.20.edge_ref), channel_id=1, source_target_pairs={{0,1},{1,0},{2,3},{3,2},{4,5},{5,4},{6,7},{7,6},{8,9},{9,8},{10,11... | collective-permute-start | bytes 393224 | tf_op jit(solution)/shard_map/ppermute | solution.py:459
  35.7 2.9 %collective-permute-done.3.other_ref = f32[4,2,4,8,128]{4,3,2,1,0:T(8,128)S(1)} collective-permute-done((f32[4,2,4,8,128]{4,3,2,1,0:T(8,128)S(1)}, f32[4,2,4,8,128]{4,3,2,1,0:T(8,128)S(1)}, u32[]{:S(2)}, u32[]{:S(2)}) %collective-permute-start.3) | collective-permute-done | bytes 131104 | tf_op jit(solution)/shard_map/ppermute | solution.py:459
  38.7 2.4 %back.1 = (f32[2,32,4096]{2,1,0:T(8,128)S(1)}, f32[2,32,4096]{2,1,0:T(8,128)S(1)}, f32[2,32,4096]{2,1,0:T(8,128)S(1)}, f32[6,32,4096]{2,1,0:T(8,128)S(1)}) custom-call(s32[9]{0:T(128)S(1)} %collective-permute-done.ints_ref, f32[6,32,4096]{2,1,0:T(8,128)S(1)} %get-tuple-element.18.window, ...), custom_call_target="tpu_custom_call", output_to_operand_aliasing={{3}: (7, {})} | custom-call | bytes 12000000 | tf_op jit(solution)/shard_map/back/pallas_call | solution.py:441
  41.0 7.2 %collective-permute-start.4 = (f32[2,32,4096]{2,1,0:T(8,128)S(1)}, f32[2,32,4096]{2,1,0:T(8,128)S(1)}, u32[]{:S(2)}, u32[]{:S(2)}) collective-permute-start(f32[2,32,4096]{2,1,0:T(8,128)S(1)} %get-tuple-element.23), channel_id=1, source_target_pairs={{0,510},{2,4},{4,2},{6,8},{8,6},{10,12},{12,10},{14,16},{16,14},{1... | collective-permute-start | bytes 3145736 | tf_op jit(solution)/shard_map/ppermute | solution.py:459
  48.2 1.9 %collective-permute-start.5 = (f32[2,32,4096]{2,1,0:T(8,128)S(1)}, f32[2,32,4096]{2,1,0:T(8,128)S(1)}, u32[]{:S(2)}, u32[]{:S(2)}) collective-permute-start(f32[2,32,4096]{2,1,0:T(8,128)S(1)} %get-tuple-element.24), channel_id=1, source_target_pairs={{0,2},{2,0},{4,6},{6,4},{8,10},{10,8},{12,14},{14,12},{16,18},{18,... | collective-permute-start | bytes 3145736 | tf_op jit(solution)/shard_map/ppermute | solution.py:459
  50.2 12.7 %collective-permute-done.4 = f32[2,32,4096]{2,1,0:T(8,128)S(1)} collective-permute-done((f32[2,32,4096]{2,1,0:T(8,128)S(1)}, f32[2,32,4096]{2,1,0:T(8,128)S(1)}, u32[]{:S(2)}, u32[]{:S(2)}) %collective-permute-start.4) | collective-permute-done | bytes 1048608 | tf_op jit(solution)/shard_map/ppermute | solution.py:459
  62.9 0.0 collective-permute-done.5
  62.9 1.1 %add_add_fusion = f32[2,32,4096]{2,1,0:T(8,128)} fusion(f32[2,32,4096]{2,1,0:T(8,128)S(1)} %collective-permute-done.5, f32[2,32,4096]{2,1,0:T(8,128)S(1)} %get-tuple-element.22, f32[2,32,4096]{2,1,0:T(8,128)S(1)} %collective-permute-done.4), kind=kLoop, calls=%fused_computation | loop fusion | flops 524288 | bytes 4194304 | tf_op jit(solution)/shard_map/add | solution.py:484
Async XLA Ops:
  0.0 29.3 %collective-permute-start.1 = (f32[2,32,4096]{2,1,0:T(8,128)}, f32[2,32,4096]{2,1,0:T(8,128)S(1)}, u32[]{:S(2)}, u32[]{:S(2)}) collective-permute-start(f32[2,32,4096]{2,1,0:T(8,128)} %own_ref.1), channel_id=1, source_target_pairs={{0,510},{2,4},{4,2},{6,8},{8,6},{10,12},{12,10},{14,16},{16,14},{1... | collective-permute-start | bytes 3145736 | tf_op jit(solution)/shard_map/ppermute | solution.py:459
  14.9 14.4 %collective-permute-start.2 = (f32[2,32,4096]{2,1,0:T(8,128)}, f32[2,32,4096]{2,1,0:T(8,128)S(1)}, u32[]{:S(2)}, u32[]{:S(2)}) collective-permute-start(f32[2,32,4096]{2,1,0:T(8,128)} %own_ref.1), channel_id=1, source_target_pairs={{0,2},{2,0},{4,6},{6,4},{8,10},{10,8},{12,14},{14,12},{16,18},{18,... | collective-permute-start | bytes 3145736 | tf_op jit(solution)/shard_map/ppermute | solution.py:459
  20.0 9.3 %collective-permute-start = (s32[9]{0:T(128)}, s32[9]{0:T(128)S(1)}, u32[]{:S(2)}, u32[]{:S(2)}) collective-permute-start(s32[9]{0:T(128)} %pack.1), channel_id=1, source_target_pairs={{0,3},{1,2},{2,5},{3,4},{4,7},{5,6},{6,9},{7,8},{8,11},{9,10},{10,... | collective-permute-start | bytes 116 | tf_op jit(solution)/shard_map/ppermute | solution.py:473
  23.4 1.2 %copy-start = (f32[2,32,4096]{2,1,0:T(8,128)S(1)}, f32[2,32,4096]{2,1,0:T(8,128)}, u32[]{:S(2)}) copy-start(f32[2,32,4096]{2,1,0:T(8,128)} %own_ref.1) | copy-start | bytes 3145732
  24.7 0.9 %copy-start.1 = (f32[52,8,128]{2,1,0:T(8,128)S(1)}, f32[52,8,128]{2,1,0:T(8,128)}, u32[]{:S(2)}) copy-start(f32[52,8,128]{2,1,0:T(8,128)} %constant.5.clone.table_ref) | copy-start | bytes 638980
  25.6 0.9 %copy-start.2 = (bf16[256,256]{1,0:T(8,128)(2,1)S(1)}, bf16[256,256]{1,0:T(8,128)(2,1)}, u32[]{:S(2)}) copy-start(bf16[256,256]{1,0:T(8,128)(2,1)} %constant.4.clone.weight_ref) | copy-start | bytes 393220
  31.2 7.5 %collective-permute-start.3 = (f32[4,2,4,8,128]{4,3,2,1,0:T(8,128)S(1)}, f32[4,2,4,8,128]{4,3,2,1,0:T(8,128)S(1)}, u32[]{:S(2)}, u32[]{:S(2)}) collective-permute-start(f32[4,2,4,8,128]{4,3,2,1,0:T(8,128)S(1)} %get-tuple-element.20.edge_ref), channel_id=1, source_target_pairs={{0,1},{1,0},{2,3},{3,2},{4,5},{5,4},{6,7},{7,6},{8,9},{9,8},{10,11... | collective-permute-start | bytes 393224 | tf_op jit(solution)/shard_map/ppermute | solution.py:459
  41.0 21.8 %collective-permute-start.4 = (f32[2,32,4096]{2,1,0:T(8,128)S(1)}, f32[2,32,4096]{2,1,0:T(8,128)S(1)}, u32[]{:S(2)}, u32[]{:S(2)}) collective-permute-start(f32[2,32,4096]{2,1,0:T(8,128)S(1)} %get-tuple-element.23), channel_id=1, source_target_pairs={{0,510},{2,4},{4,2},{6,8},{8,6},{10,12},{12,10},{14,16},{16,14},{1... | collective-permute-start | bytes 3145736 | tf_op jit(solution)/shard_map/ppermute | solution.py:459
  48.2 14.6 %collective-permute-start.5 = (f32[2,32,4096]{2,1,0:T(8,128)S(1)}, f32[2,32,4096]{2,1,0:T(8,128)S(1)}, u32[]{:S(2)}, u32[]{:S(2)}) collective-permute-start(f32[2,32,4096]{2,1,0:T(8,128)S(1)} %get-tuple-element.24), channel_id=1, source_target_pairs={{0,2},{2,0},{4,6},{6,4},{8,10},{10,8},{12,14},{14,12},{16,18},{18,... | collective-permute-start | bytes 3145736 | tf_op jit(solution)/shard_map/ppermute | solution.py:459

commit v4 on v3

--- a/solution.py
+++ b/solution.py
@@ -454,6 +454,35 @@
     )(ints, window, local, edges, other, weights, table, result)
 
 
+def finish_kernel(own_ref, cross_ref, mate_ref, out_ref, total, sems):
+    copies = []
+    for n in range(2):
+        for o in range(total.shape[1] // 8):
+            span = pl.ds(8 * o, 8)
+            total[n, span] = (own_ref[n, span] + cross_ref[n, span]) + mate_ref[n, span]
+            copies.append(pltpu.make_async_copy(
+                total.at[n, span], out_ref.at[n, span], sems.at[n, o]
+            ))
+            copies[-1].start()
+    for copy in copies:
+        copy.wait()
+
+
+def finish(own, cross, mate):
+    return pl.pallas_call(
+        finish_kernel,
+        out_shape=jax.ShapeDtypeStruct(own.shape, jnp.float32),
+        in_specs=[VMEM, VMEM, VMEM],
+        out_specs=HBM,
+        scratch_shapes=[
+            pltpu.VMEM(own.shape, jnp.float32),
+            pltpu.SemaphoreType.DMA((2, own.shape[1] // 8)),
+        ],
+        compiler_params=LIMIT,
+        name="finish",
+    )(own, cross, mate)
+
+
 def moved(value, axis, target):
     count = lax.axis_size(axis)
     return lax.ppermute(value, axis, [(n, target(n) % count) for n in range(count)])
@@ -481,7 +510,7 @@
     local, edges, window = forward(ints, cross, mate, window, weights, table)
     other = moved(edges, "grid", lambda n: n + 1)
     cross, mate, own, _ = back(ints, window, local, edges, other, weights, table, result)
-    return (own + to_cross(cross)) + to_mate(mate)
+    return finish(own, to_cross(cross), to_mate(mate))
 
 
 def solution(mesh):

time: 65 us -> 65.6 us (level); the launches traced: 64 us -> 66.5 us
  starting transfers between devices: 33.9 us -> 28.7 us
  waiting for transfers between devices: 17.7 us -> 22.8 us
  Pallas kernels: 6.18 us -> 9.78 us
  other arithmetic: 1.12 us -> 0 us
    ppermute x5, waiting for transfers between devices: 15.6 us -> 20.8 us  [moved(): lax.ppermute(value, axis, [(n, target(n) % count) for n in range(count)])]
    ppermute x5, starting transfers between devices: 30.5 us -> 25.3 us  [moved(): lax.ppermute(value, axis, [(n, target(n) % count) for n in range(count)])]
    pallas_call x1, Pallas kernels: 2.35 us -> 3.87 us  [back(): pl.pallas_call(back_kernel, out_shape=(block, block, block, jax.ShapeDtyp...]
    add x1 -> x0, other arithmetic: 1.12 us -> none  [on_device(): return own + to_cross(cross) + to_mate(mate)]
    pallas_call x0 -> x1, Pallas kernels: none -> 1.05 us  [finish(): pl.pallas_call(finish_kernel, out_shape=jax.ShapeDtypeStruct(own.shape, j...]
    pallas_call x1, Pallas kernels: 1.88 us -> 2.91 us  [forward(): pl.pallas_call(forward_kernel, out_shape=(jax.ShapeDtypeStruct((4, GROUPS...]
where the time goes in v4:
time: 65.6 us; the launch traced here: 66.5 us
  starting transfers between devices  28.7 us (44%)
  waiting for transfers between devices  22.8 us (35%)
  Pallas kernels  9.78 us (15%)
  local copies, waits for them, and re-layouts  4.39 us (7%)
  between operations  0.74 us (1%)
    ppermute x5, starting transfers between devices, moved(): lax.ppermute(value, axis, [(n, target(n) % count) for n in range(count)])  25.3 us
    ppermute x5, waiting for transfers between devices, moved(): lax.ppermute(value, axis, [(n, target(n) % count) for n in range(count)])  20.8 us
    unnamed x7, local copies, waits for them, and re-layouts  4.39 us
    pallas_call x1, Pallas kernels, back(): pl.pallas_call(back_kernel, out_shape=(block, block, block, jax.ShapeDtyp...  3.87 us
    ppermute x1, starting transfers between devices, to_next_other_slab(): return lax.ppermute(value, ('band', 'grid'), pairs)  3.44 us
    pallas_call x1, Pallas kernels, forward(): pl.pallas_call(forward_kernel, out_shape=(jax.ShapeDtypeStruct((4, GROUPS...  2.91 us
    ppermute x1, waiting for transfers between devices, to_next_other_slab(): return lax.ppermute(value, ('band', 'grid'), pairs)  2.02 us
  transfers between devices with their start and end apart: 6, of which 3 were waited for; matrix products, arithmetic and copies ran while one was open for 2% of the time, Pallas kernels for 3%

profile of v4, /device:TPU:2, one launch (start us, length us, event | category | flops | bytes accessed | tf_op | source)
XLA Modules:
  0.0 66.5 jit_solution(2691504212319962792)
XLA Ops:
  0.0 14.8 %collective-permute-start.1 = (f32[2,32,4096]{2,1,0:T(8,128)}, f32[2,32,4096]{2,1,0:T(8,128)S(1)}, u32[]{:S(2)}, u32[]{:S(2)}) collective-permute-start(f32[2,32,4096]{2,1,0:T(8,128)} %own_ref.1), channel_id=1, source_target_pairs={{0,510},{2,4},{4,2},{6,8},{8,6},{10,12},{12,10},{14,16},{16,14},{1... | collective-permute-start | bytes 3145736 | tf_op jit(solution)/shard_map/ppermute | solution.py:488
  14.9 1.9 %collective-permute-start.2 = (f32[2,32,4096]{2,1,0:T(8,128)}, f32[2,32,4096]{2,1,0:T(8,128)S(1)}, u32[]{:S(2)}, u32[]{:S(2)}) collective-permute-start(f32[2,32,4096]{2,1,0:T(8,128)} %own_ref.1), channel_id=1, source_target_pairs={{0,2},{2,0},{4,6},{6,4},{8,10},{10,8},{12,14},{14,12},{16,18},{18,... | collective-permute-start | bytes 3145736 | tf_op jit(solution)/shard_map/ppermute | solution.py:488
  17.4 1.3 %copy.8.pairs_ref = s32[1,4,2]{2,1,0:T(4,128)} copy(s32[1,4,2]{1,2,0:T(2,128)} %param.6) | data formatting | bytes 64 | tf_op args[1]
  18.8 1.2 %pack.1 = s32[9]{0:T(128)} custom-call(s32[1,4,2]{2,1,0:T(4,128)} %copy.8.pairs_ref, s32[1]{0:T(128)S(6)} %copy.11.count_ref), custom_call_target="tpu_custom_call" | custom-call | tf_op jit(solution)/shard_map/pack/pallas_call | solution.py:388
  20.0 3.4 %collective-permute-start = (s32[9]{0:T(128)}, s32[9]{0:T(128)S(1)}, u32[]{:S(2)}, u32[]{:S(2)}) collective-permute-start(s32[9]{0:T(128)} %pack.1), channel_id=1, source_target_pairs={{0,3},{1,2},{2,5},{3,4},{4,7},{5,6},{6,9},{7,8},{8,11},{9,10},{10,... | collective-permute-start | bytes 116 | tf_op jit(solution)/shard_map/ppermute | solution.py:502
  23.4 0.0 copy-start
  23.4 1.2 %copy-done = f32[2,32,4096]{2,1,0:T(8,128)S(1)} copy-done((f32[2,32,4096]{2,1,0:T(8,128)S(1)}, f32[2,32,4096]{2,1,0:T(8,128)}, u32[]{:S(2)}) %copy-start) | copy-done | bytes 1048600
  24.7 0.0 copy-start.1
  24.7 0.9 %copy-done.1 = f32[52,8,128]{2,1,0:T(8,128)S(1)} copy-done((f32[52,8,128]{2,1,0:T(8,128)S(1)}, f32[52,8,128]{2,1,0:T(8,128)}, u32[]{:S(2)}) %copy-start.1) | copy-done | bytes 213016
  25.6 0.0 copy-start.2
  25.6 0.9 %copy-done.2 = bf16[256,256]{1,0:T(8,128)(2,1)S(1)} copy-done((bf16[256,256]{1,0:T(8,128)(2,1)S(1)}, bf16[256,256]{1,0:T(8,128)(2,1)}, u32[]{:S(2)}) %copy-start.2) | copy-done | bytes 131096
  26.5 0.7 %prepare.1 = (f32[6,32,4096]{2,1,0:T(8,128)S(1)}, f32[6,32,4096]{2,1,0:T(8,128)S(1)}, bf16[256,256]{1,0:T(8,128)(2,1)S(1)}, f32[52,8,128]{2,1,0:T(8,128)S(1)}) custom-call(f32[2,32,4096]{2,1,0:T(8,128)S(1)} %copy-done, bf16[256,256]{1,0:T(8,128)(2,1)S(1)} %copy-done.2, f32[52,8,128]{2,1,0:T(8,128)S(1)} %copy-done.1), custom_call_target="tpu_custom_call" | custom-call | bytes 12000000 | tf_op jit(solution)/shard_map/prepare/pallas_call | solution.py:399
  27.3 2.0 %collective-permute-done.ints_ref = s32[9]{0:T(128)S(1)} collective-permute-done((s32[9]{0:T(128)}, s32[9]{0:T(128)S(1)}, u32[]{:S(2)}, u32[]{:S(2)}) %collective-permute-start) | collective-permute-done | bytes 68 | tf_op jit(solution)/shard_map/ppermute | solution.py:502
  29.3 0.0 collective-permute-done.1.cross_ref
  29.3 0.0 collective-permute-done.2.mate_ref
  29.3 2.9 %forward.1 = (f32[4,4,32,8,128]{4,3,2,1,0:T(8,128)S(1)}, f32[4,2,4,8,128]{4,3,2,1,0:T(8,128)S(1)}, f32[6,32,4096]{2,1,0:T(8,128)S(1)}) custom-call(s32[9]{0:T(128)S(1)} %collective-permute-done.ints_ref, f32[2,32,4096]{2,1,0:T(8,128)S(1)} %collective-permute-done.1.cross_ref, ...), custom_call_target="tpu_custom_call", output_to_operand_aliasing={{2}: (3, {})} | custom-call | bytes 12000000 | tf_op jit(solution)/shard_map/forward/pallas_call | solution.py:418
  32.2 4.6 %collective-permute-start.3 = (f32[4,2,4,8,128]{4,3,2,1,0:T(8,128)S(1)}, f32[4,2,4,8,128]{4,3,2,1,0:T(8,128)S(1)}, u32[]{:S(2)}, u32[]{:S(2)}) collective-permute-start(f32[4,2,4,8,128]{4,3,2,1,0:T(8,128)S(1)} %get-tuple-element.20.edge_ref), channel_id=1, source_target_pairs={{0,1},{1,0},{2,3},{3,2},{4,5},{5,4},{6,7},{7,6},{8,9},{9,8},{10,11... | collective-permute-start | bytes 393224 | tf_op jit(solution)/shard_map/ppermute | solution.py:488
  36.8 2.9 %collective-permute-done.3.other_ref = f32[4,2,4,8,128]{4,3,2,1,0:T(8,128)S(1)} collective-permute-done((f32[4,2,4,8,128]{4,3,2,1,0:T(8,128)S(1)}, f32[4,2,4,8,128]{4,3,2,1,0:T(8,128)S(1)}, u32[]{:S(2)}, u32[]{:S(2)}) %collective-permute-start.3) | collective-permute-done | bytes 131104 | tf_op jit(solution)/shard_map/ppermute | solution.py:488
  39.7 3.9 %back.1 = (f32[2,32,4096]{2,1,0:T(8,128)S(1)}, f32[2,32,4096]{2,1,0:T(8,128)S(1)}, f32[2,32,4096]{2,1,0:T(8,128)S(1)}, f32[6,32,4096]{2,1,0:T(8,128)S(1)}) custom-call(s32[9]{0:T(128)S(1)} %collective-permute-done.ints_ref, f32[6,32,4096]{2,1,0:T(8,128)S(1)} %get-tuple-element.18.window, ...), custom_call_target="tpu_custom_call", output_to_operand_aliasing={{3}: (7, {})} | custom-call | bytes 12000000 | tf_op jit(solution)/shard_map/back/pallas_call | solution.py:441
  43.6 2.0 %collective-permute-start.4 = (f32[2,32,4096]{2,1,0:T(8,128)S(1)}, f32[2,32,4096]{2,1,0:T(8,128)S(1)}, u32[]{:S(2)}, u32[]{:S(2)}) collective-permute-start(f32[2,32,4096]{2,1,0:T(8,128)S(1)} %get-tuple-element.23), channel_id=1, source_target_pairs={{0,510},{2,4},{4,2},{6,8},{8,6},{10,12},{12,10},{14,16},{16,14},{1... | collective-permute-start | bytes 3145736 | tf_op jit(solution)/shard_map/ppermute | solution.py:488
  45.6 1.9 %collective-permute-start.5 = (f32[2,32,4096]{2,1,0:T(8,128)S(1)}, f32[2,32,4096]{2,1,0:T(8,128)S(1)}, u32[]{:S(2)}, u32[]{:S(2)}) collective-permute-start(f32[2,32,4096]{2,1,0:T(8,128)S(1)} %get-tuple-element.24), channel_id=1, source_target_pairs={{0,2},{2,0},{4,6},{6,4},{8,10},{10,8},{12,14},{14,12},{16,18},{18,... | collective-permute-start | bytes 3145736 | tf_op jit(solution)/shard_map/ppermute | solution.py:488
  47.6 17.9 %collective-permute-done.4.cross_ref = f32[2,32,4096]{2,1,0:T(8,128)S(1)} collective-permute-done((f32[2,32,4096]{2,1,0:T(8,128)S(1)}, f32[2,32,4096]{2,1,0:T(8,128)S(1)}, u32[]{:S(2)}, u32[]{:S(2)}) %collective-permute-start.4) | collective-permute-done | bytes 1048608 | tf_op jit(solution)/shard_map/ppermute | solution.py:488
  65.4 0.0 collective-permute-done.5.mate_ref
  65.4 1.0 %finish.1 = f32[2,32,4096]{2,1,0:T(8,128)} custom-call(f32[2,32,4096]{2,1,0:T(8,128)S(1)} %get-tuple-element.22.own_ref, f32[2,32,4096]{2,1,0:T(8,128)S(1)} %collective-permute-done.4.cross_ref, f32[2,32,4096]{2,1,0:T(8,128)S(1)} %collective-permute-done.5.mate_ref), custom_call_target="tpu_custom_call" | custom-call | tf_op jit(solution)/shard_map/finish/pallas_call | solution.py:472
Async XLA Ops:
  0.0 29.3 %collective-permute-start.1 = (f32[2,32,4096]{2,1,0:T(8,128)}, f32[2,32,4096]{2,1,0:T(8,128)S(1)}, u32[]{:S(2)}, u32[]{:S(2)}) collective-permute-start(f32[2,32,4096]{2,1,0:T(8,128)} %own_ref.1), channel_id=1, source_target_pairs={{0,510},{2,4},{4,2},{6,8},{8,6},{10,12},{12,10},{14,16},{16,14},{1... | collective-permute-start | bytes 3145736 | tf_op jit(solution)/shard_map/ppermute | solution.py:488
  14.9 14.4 %collective-permute-start.2 = (f32[2,32,4096]{2,1,0:T(8,128)}, f32[2,32,4096]{2,1,0:T(8,128)S(1)}, u32[]{:S(2)}, u32[]{:S(2)}) collective-permute-start(f32[2,32,4096]{2,1,0:T(8,128)} %own_ref.1), channel_id=1, source_target_pairs={{0,2},{2,0},{4,6},{6,4},{8,10},{10,8},{12,14},{14,12},{16,18},{18,... | collective-permute-start | bytes 3145736 | tf_op jit(solution)/shard_map/ppermute | solution.py:488
  20.0 9.3 %collective-permute-start = (s32[9]{0:T(128)}, s32[9]{0:T(128)S(1)}, u32[]{:S(2)}, u32[]{:S(2)}) collective-permute-start(s32[9]{0:T(128)} %pack.1), channel_id=1, source_target_pairs={{0,3},{1,2},{2,5},{3,4},{4,7},{5,6},{6,9},{7,8},{8,11},{9,10},{10,... | collective-permute-start | bytes 116 | tf_op jit(solution)/shard_map/ppermute | solution.py:502
  23.4 1.2 %copy-start = (f32[2,32,4096]{2,1,0:T(8,128)S(1)}, f32[2,32,4096]{2,1,0:T(8,128)}, u32[]{:S(2)}) copy-start(f32[2,32,4096]{2,1,0:T(8,128)} %own_ref.1) | copy-start | bytes 3145732
  24.7 0.9 %copy-start.1 = (f32[52,8,128]{2,1,0:T(8,128)S(1)}, f32[52,8,128]{2,1,0:T(8,128)}, u32[]{:S(2)}) copy-start(f32[52,8,128]{2,1,0:T(8,128)} %constant.5.clone.table_ref) | copy-start | bytes 638980
  25.6 0.9 %copy-start.2 = (bf16[256,256]{1,0:T(8,128)(2,1)S(1)}, bf16[256,256]{1,0:T(8,128)(2,1)}, u32[]{:S(2)}) copy-start(bf16[256,256]{1,0:T(8,128)(2,1)} %constant.4.clone.weight_ref) | copy-start | bytes 393220
  32.2 7.5 %collective-permute-start.3 = (f32[4,2,4,8,128]{4,3,2,1,0:T(8,128)S(1)}, f32[4,2,4,8,128]{4,3,2,1,0:T(8,128)S(1)}, u32[]{:S(2)}, u32[]{:S(2)}) collective-permute-start(f32[4,2,4,8,128]{4,3,2,1,0:T(8,128)S(1)} %get-tuple-element.20.edge_ref), channel_id=1, source_target_pairs={{0,1},{1,0},{2,3},{3,2},{4,5},{5,4},{6,7},{7,6},{8,9},{9,8},{10,11... | collective-permute-start | bytes 393224 | tf_op jit(solution)/shard_map/ppermute | solution.py:488
  43.6 21.8 %collective-permute-start.4 = (f32[2,32,4096]{2,1,0:T(8,128)S(1)}, f32[2,32,4096]{2,1,0:T(8,128)S(1)}, u32[]{:S(2)}, u32[]{:S(2)}) collective-permute-start(f32[2,32,4096]{2,1,0:T(8,128)S(1)} %get-tuple-element.23), channel_id=1, source_target_pairs={{0,510},{2,4},{4,2},{6,8},{8,6},{10,12},{12,10},{14,16},{16,14},{1... | collective-permute-start | bytes 3145736 | tf_op jit(solution)/shard_map/ppermute | solution.py:488
  45.6 19.8 %collective-permute-start.5 = (f32[2,32,4096]{2,1,0:T(8,128)S(1)}, f32[2,32,4096]{2,1,0:T(8,128)S(1)}, u32[]{:S(2)}, u32[]{:S(2)}) collective-permute-start(f32[2,32,4096]{2,1,0:T(8,128)S(1)} %get-tuple-element.24), channel_id=1, source_target_pairs={{0,2},{2,0},{4,6},{6,4},{8,10},{10,8},{12,14},{14,12},{16,18},{18,... | collective-permute-start | bytes 3145736 | tf_op jit(solution)/shard_map/ppermute | solution.py:488
